TPU v7x, 32 devices: a whole 2x2x4 slice. The times are simulated.
32 devices in a mesh: pts: 4 (over y, core), cen: 8 (over z, x).
Axes of the slice: x: 2, y: 2, z: 4, core: 2. Of those that a mesh axis runs over, the one named last changes fastest.
Arguments:
- points: bfloat16 [16384, 1024], P('pts'), may hold values from -128 to 128
- centroids: float32 [8192, 1024], P('cen'), may hold values from -10 to 10
Outputs:
- centroid_means: float32 [8192, 1024], P('cen', 'pts')
- log_norms: float32 [16384], P('pts')
All inputs are finite; a program needn't handle non-finite values.
Results may differ from a plain program's by a relative error of at most 0.0015.
The roundings to bfloat16 on the way count: a program that leaves them out, or rounds other values in their place, can miss the bound.
Values may be sent and summed in bfloat16 or wider, within the bound.
No kernel may reach another device: no remote copies, remote signals or barrier semaphores. Data moves between devices by JAX's collectives and lax.ppermute only.
A program may use at most 64 MiB of HBM per device.

v0:
```python
import jax
import jax.numpy as jnp
from jax import lax
from jax.sharding import PartitionSpec as P

ITERS = 2


def normalize_rows(rows, square_sums):
    return rows * lax.rsqrt(square_sums + 1e-06)[:, None]


def on_device(points, centroids):
    unit_rows = normalize_rows(centroids, jnp.sum(centroids * centroids, axis=1)).astype(
        jnp.bfloat16
    )
    ones_row = jnp.ones((1, points.shape[0]), jnp.bfloat16)
    centroid_means = centroids
    log_norms = jnp.zeros((points.shape[0],), jnp.float32)
    for iteration in range(ITERS):
        final_step = iteration + 1 == ITERS
        logits = lax.dot_general(
            points, unit_rows, (((1,), (1,)), ((), ())), preferred_element_type=jnp.float32
        )
        local_max = jnp.max(logits, axis=1)
        row_max = lax.pmax(local_max, "cen")
        shifted = jnp.exp(logits - row_max[:, None])
        row_total = lax.psum(jnp.sum(shifted, axis=1), "cen")
        weights = (shifted / row_total[:, None]).astype(jnp.bfloat16)
        log_norms = row_max + jnp.log(row_total)
        weighted = lax.dot_general(
            weights, points, (((0,), (0,)), ((), ())), preferred_element_type=jnp.float32
        )
        point_mass = jnp.dot(ones_row, weights, preferred_element_type=jnp.float32)[0]
        shares = lax.psum_scatter(weighted, "pts", scatter_dimension=1, tiled=True)
        point_mass = lax.psum(point_mass, "pts")
        centroid_means = shares / jnp.maximum(point_mass, 1.0)[:, None]
        if not final_step:
            square_sums = lax.psum(jnp.sum(centroid_means * centroid_means, axis=1), "pts")
            unit_shares = normalize_rows(centroid_means, square_sums).astype(jnp.bfloat16)
            unit_rows = lax.all_gather(unit_shares, "pts", axis=1, tiled=True)
    return (centroid_means, log_norms)


def solution(mesh):
    placed = (P("pts", None), P("cen", None))
    return jax.shard_map(
        on_device,
        mesh=mesh,
        in_specs=placed,
        out_specs=(P("cen", "pts"), P("pts")),
        check_vma=False,
    )
```

profile of v0, /device:TPU:0, one launch (start us, length us, event | category | flops | bytes accessed | tf_op | source)
XLA Modules:
  0.0 371.7 jit_solution(13198026236314286153)
XLA Ops:
  7.2 0.0 reduce-scatter.3.cloned.1.call-start
  7.2 2.5 multiply_reduce_fusion
  9.8 15.8 %fusion.12 = (f32[4096]{0:T(1024)S(1)}, f32[1024,4096]{1,0:T(8,128)}) fusion(bf16[4096,1024]{1,0:T(8,128)(2,1)} %param.2, f32[1024,1024]{1,0:T(8,128)} %param.3, f32[1024]{0:T(1024)S(1)} %add_rsqrt_fusion.1), kind=kOutput, calls=%fused_computation.27 | convolution fusion | flops 8596221952 | bytes 29380608 | tf_op jit(solution)/shard_map/dot_general | solution.py:22
  25.6 38.8 %pmax.14 = f32[4096]{0:T(1024)S(1)} all-reduce(f32[4096]{0:T(1024)S(1)} %get-tuple-element.2), channel_id=1, replica_groups=mesh['pts'=4,'cen'=8] {'cen'}, use_global_device_ids=true, to_apply=%region_2.0 | all-reduce | flops 4096 | bytes 32768 | tf_op jit(solution)/shard_map/pmax | solution.py:26
  64.4 8.0 %fusion = f32[4096]{0:T(1024)S(1)} fusion(f32[1024,4096]{1,0:T(8,128)} %get-tuple-element.3, f32[4096]{0:T(1024)S(1)} %pmax.14), kind=kLoop, calls=%fused_computation.4 | loop fusion | flops 8384512 | bytes 16809984 | tf_op jit(solution)/shard_map/reduce_sum | solution.py:28
  72.4 33.0 %psum.35 = f32[4096]{0:T(1024)S(1)} all-reduce(f32[4096]{0:T(1024)S(1)} %fusion), channel_id=1, replica_groups=mesh['pts'=4,'cen'=8] {'cen'}, use_global_device_ids=true, to_apply=%region_4.0 | all-reduce | flops 4096 | bytes 32768 | tf_op jit(solution)/shard_map/psum | solution.py:28
  105.4 7.4 %divide_convert_fusion.1 = bf16[1024,4096]{1,0:T(8,128)(2,1)S(1)} fusion(f32[1024,4096]{1,0:T(8,128)} %get-tuple-element.3, f32[4096]{0:T(1024)S(1)} %psum.35, f32[4096]{0:T(1024)S(1)} %pmax.14), kind=kLoop, calls=%fused_computation.2 | loop fusion | flops 12582912 | bytes 25198592 | tf_op jit(solution)/shard_map/convert_element_type | solution.py:29
  112.8 0.0 copy-start
  112.8 3.2 copy-done
  116.0 12.5 %fusion.14 = f32[1024,1024]{1,0:T(8,128)} fusion(bf16[1024,4096]{1,0:T(8,128)(2,1)S(1)} %divide_convert_fusion.1, bf16[4096,1024]{1,0:T(8,128)(2,1)} %param.2), kind=kOutput, calls=%fused_computation.29 | convolution fusion | flops 8589934592 | bytes 20971520 | tf_op jit(solution)/shard_map/dot_general | solution.py:31
  128.5 0.0 reduce-scatter.3.cloned.1.call-update
  128.5 0.2 all-gather.2.cloned.1.call-start
  128.8 6.3 %fusion.4 = f32[1,1024]{1,0:T(1,128)S(1)} fusion(bf16[1024,4096]{1,0:T(8,128)(2,1)} %copy-done), kind=kOutput, calls=%fused_computation.8 | convolution fusion | flops 8388608 | bytes 8392704 | tf_op jit(solution)/shard_map/dot_general | solution.py:34
  135.1 5.6 %psum.36 = f32[1024]{0:T(1024)S(1)} all-reduce(f32[1024]{0:T(1024)S(1)} %bitcast.15), channel_id=1, replica_groups=mesh['pts'=4,'cen'=8] {'pts'}, use_global_device_ids=true, to_apply=%region_6.0 | all-reduce | flops 1024 | bytes 8192 | tf_op jit(solution)/shard_map/psum | solution.py:36
  140.7 29.7 %reduce-scatter.3.cloned.1.call-done = f32[1024,256]{1,0:T(8,128)} async-done(((f32[1024,1024]{1,0:T(8,128)}), f32[1024,256]{1,0:T(8,128)}) %reduce-scatter.3.cloned.1.call-update) | async-done | bytes 1048592 | tf_op jit(solution)/shard_map/reduce_scatter | solution.py:35
  170.5 1.6 multiply_reduce_fusion.1
  172.1 5.8 %psum.37 = f32[1024]{0:T(1024)S(1)} all-reduce(f32[1024]{0:T(1024)S(1)} %multiply_reduce_fusion.1), channel_id=1, replica_groups=mesh['pts'=4,'cen'=8] {'pts'}, use_global_device_ids=true, to_apply=%region_8.0 | all-reduce | flops 1024 | bytes 8192 | tf_op jit(solution)/shard_map/psum | solution.py:39
  177.8 2.4 multiply_convert_fusion.2
  180.2 0.0 all-gather.2.cloned.1.call-update
  180.2 0.0 reduce-scatter.5.cloned.1.call-start
  180.3 24.0 %all-gather.2.cloned.1.call-done = bf16[1024,1024]{1,0:T(8,128)(2,1)} async-done(((bf16[1024,256]{1,0:T(8,128)(2,1)}), bf16[1024,1024]{1,0:T(8,128)(2,1)}) %all-gather.2.cloned.1.call-update) | async-done | bytes 2097168 | tf_op jit(solution)/shard_map/all_gather | solution.py:41
  204.3 16.0 %fusion.13 = (f32[4096]{0:T(1024)S(1)}, f32[1024,4096]{1,0:T(8,128)}) fusion(bf16[1024,1024]{1,0:T(8,128)(2,1)} %all-gather.2.cloned.1.call-done, bf16[4096,1024]{1,0:T(8,128)(2,1)} %param.2), kind=kOutput, calls=%fused_computation.28 | convolution fusion | flops 8594124800 | bytes 27279360 | tf_op jit(solution)/shard_map/dot_general | solution.py:22
  220.4 37.1 %pmax.15 = f32[4096]{0:T(1024)S(1)} all-reduce(f32[4096]{0:T(1024)S(1)} %get-tuple-element.4), channel_id=1, replica_groups=mesh['pts'=4,'cen'=8] {'cen'}, use_global_device_ids=true, to_apply=%region_10.0 | all-reduce | flops 4096 | bytes 32768 | tf_op jit(solution)/shard_map/pmax | solution.py:26
  257.4 8.0 %fusion.1 = f32[4096]{0:T(1024)S(1)} fusion(f32[1024,4096]{1,0:T(8,128)} %get-tuple-element.5, f32[4096]{0:T(1024)S(1)} %pmax.15), kind=kLoop, calls=%fused_computation.5 | loop fusion | flops 8384512 | bytes 16809984 | tf_op jit(solution)/shard_map/reduce_sum | solution.py:28
  265.4 33.2 %psum.38 = f32[4096]{0:T(1024)S(1)} all-reduce(f32[4096]{0:T(1024)S(1)} %fusion.1), channel_id=1, replica_groups=mesh['pts'=4,'cen'=8] {'cen'}, use_global_device_ids=true, to_apply=%region_12.0 | all-reduce | flops 4096 | bytes 32768 | tf_op jit(solution)/shard_map/psum | solution.py:28
  298.6 7.4 %divide_convert_fusion = bf16[1024,4096]{1,0:T(8,128)(2,1)S(1)} fusion(f32[1024,4096]{1,0:T(8,128)} %get-tuple-element.5, f32[4096]{0:T(1024)S(1)} %psum.38, f32[4096]{0:T(1024)S(1)} %pmax.15), kind=kLoop, calls=%fused_computation | loop fusion | flops 12582912 | bytes 25198592 | tf_op jit(solution)/shard_map/convert_element_type | solution.py:29
  306.0 0.0 copy-start.1
  306.1 3.2 copy-done.1
  309.3 12.5 %fusion.15 = f32[1024,1024]{1,0:T(8,128)} fusion(bf16[1024,4096]{1,0:T(8,128)(2,1)S(1)} %divide_convert_fusion, bf16[4096,1024]{1,0:T(8,128)(2,1)} %param.2), kind=kOutput, calls=%fused_computation.30 | convolution fusion | flops 8589934592 | bytes 20971520 | tf_op jit(solution)/shard_map/dot_general | solution.py:31
  321.8 0.0 reduce-scatter.5.cloned.1.call-update
  321.8 6.3 %fusion.2 = f32[1,1024]{1,0:T(1,128)S(1)} fusion(bf16[1024,4096]{1,0:T(8,128)(2,1)} %copy-done.1), kind=kOutput, calls=%fused_computation.6 | convolution fusion | flops 8388608 | bytes 8392704 | tf_op jit(solution)/shard_map/dot_general | solution.py:34
  328.1 5.7 %psum.39 = f32[1024]{0:T(1024)S(1)} all-reduce(f32[1024]{0:T(1024)S(1)} %bitcast.16), channel_id=1, replica_groups=mesh['pts'=4,'cen'=8] {'pts'}, use_global_device_ids=true, to_apply=%region_14.0 | all-reduce | flops 1024 | bytes 8192 | tf_op jit(solution)/shard_map/psum | solution.py:36
  333.9 0.6 log_add_fusion
  334.5 28.2 %reduce-scatter.5.cloned.1.call-done = f32[1024,256]{1,0:T(8,128)} async-done(((f32[1024,1024]{1,0:T(8,128)}), f32[1024,256]{1,0:T(8,128)}) %reduce-scatter.5.cloned.1.call-update) | async-done | bytes 1048592 | tf_op jit(solution)/shard_map/reduce_scatter | solution.py:35
  362.7 2.4 broadcast_divide_fusion
  (4 shorter events, 0.0 us)
Async XLA Ops:
  7.2 163.3 %reduce-scatter.3.cloned.1.call-start = ((), (), s32[]{:S(2)}) async-start(), calls=%async_computation.2 | async-start | bytes 5242880 | tf_op jit(solution)/shard_map/reduce_scatter | solution.py:35
  112.8 3.2 copy-start
  128.5 75.8 %all-gather.2.cloned.1.call-start = ((), (), s32[]{:S(2)}) async-start(), calls=%async_computation.3 | async-start | bytes 2621440 | tf_op jit(solution)/shard_map/all_gather | solution.py:41
  180.2 182.5 %reduce-scatter.5.cloned.1.call-start = ((), (), s32[]{:S(2)}) async-start(), calls=%async_computation.4 | async-start | bytes 5242880 | tf_op jit(solution)/shard_map/reduce_scatter | solution.py:35
  306.0 3.2 copy-start.1
Sparse Core Ops, SparseCore 0:
  128.7 41.7 reduce-scatter.2
  180.4 23.9 all-gather.1
  321.9 40.7 reduce-scatter.4
where the time goes:
time: 372 us
  blocking collectives  159 us (43%)
  waiting for transfers between devices  82.1 us (22%)
  matrix products  69.5 us (19%)
  other arithmetic  40.3 us (11%)
  between operations  13.8 us (4%)
  local copies, waits for them, and re-layouts  6.43 us (2%)
    pmax x2, blocking collectives, on_device(): row_max = lax.pmax(local_max, 'cen')  75.9 us
    psum x2, blocking collectives, on_device(): row_total = lax.psum(jnp.sum(shifted, axis=1), 'cen')  66.2 us
    reduce_scatter x2, waiting for transfers between devices, on_device(): shares = lax.psum_scatter(weighted, 'pts', scatter_dimension=1, tiled=True)  58 us
    dot_general x2, matrix products, on_device(): lax.dot_general(points, unit_rows, (((1,), (1,)), ((), ())), preferred_el...  31.9 us
    dot_general x2, matrix products, on_device(): lax.dot_general(weights, points, (((0,), (0,)), ((), ())), preferred_elem...  25 us
    all_gather x1, waiting for transfers between devices, on_device(): unit_rows = lax.all_gather(unit_shares, 'pts', axis=1, tiled=True)  24 us
    reduce_sum x2, other arithmetic, on_device(): row_total = lax.psum(jnp.sum(shifted, axis=1), 'cen')  16 us
    convert_element_type x2, other arithmetic, on_device(): weights = (shifted / row_total[:, None]).astype(jnp.bfloat16)  14.8 us
  transfers between devices with their start and end apart: 3, of which 3 were waited for; matrix products, arithmetic and copies ran while one was open for 4% of the time, Pallas kernels for 0%

commit v1 on v0

v1 whole, which is shorter than its diff:
```python
import functools

import jax
import jax.numpy as jnp
from jax import lax
from jax.experimental import pallas as pl
from jax.experimental.pallas import tpu as pltpu
from jax.sharding import PartitionSpec as P

ITERS = 2
F32 = jnp.float32
BF16 = jnp.bfloat16
VMEM_LIMIT = 40 * 2**20


def divisor(total, wanted):
    size = min(total, wanted)
    while total % size:
        size -= 1
    return size


def normalize_rows(rows):
    return rows * lax.rsqrt(jnp.sum(rows * rows, axis=1, keepdims=True) + 1e-06)


def fill_from_centroids(pos_ref, unit_refs, units):
    rows = units.shape[0]
    step = divisor(rows, 256)
    for start in range(0, rows, step):
        block = unit_refs[0][start : start + step, :]
        units[start : start + step, :] = normalize_rows(block).astype(BF16)


def fill_from_blocks(pos_ref, unit_refs, units):
    rows = unit_refs[0].shape[0]
    for number, ref in enumerate(unit_refs):
        start = pl.multiple_of(pos_ref[number] * rows, rows)
        units[pl.ds(start, rows), :] = ref[...]


def score_body(fill, count, sub, pos_ref, *refs):
    unit_refs = refs[:count]
    x_ref, e_ref, stat_ref, units = refs[count:]

    @pl.when(pl.program_id(0) == 0)
    def _():
        fill(pos_ref, unit_refs, units)

    for start in range(0, x_ref.shape[0], sub):
        part = slice(start, start + sub)
        logits = lax.dot_general(
            units[...], x_ref[part, :], (((1,), (1,)), ((), ())), preferred_element_type=F32
        )
        top = jnp.max(logits, axis=0, keepdims=True)
        shifted = jnp.exp(logits - top)
        e_ref[:, part] = shifted
        stat_ref[0:1, part] = top
        stat_ref[1:2, part] = jnp.sum(shifted, axis=0, keepdims=True)


def scores(fill, pos, unit_arrays, points, rows):
    total, width = points.shape
    block = divisor(total, 512)
    sub = divisor(block, 256)
    whole = [
        pl.BlockSpec(u.shape, lambda i, pos: (0, 0), pipeline_mode=pl.Buffered(1)) for u in unit_arrays
    ]
    return pl.pallas_call(
        functools.partial(score_body, fill, len(unit_arrays), sub),
        grid_spec=pltpu.PrefetchScalarGridSpec(
            num_scalar_prefetch=1,
            grid=(total // block,),
            in_specs=whole + [pl.BlockSpec((block, width), lambda i, pos: (i, 0))],
            out_specs=[
                pl.BlockSpec((rows, block), lambda i, pos: (0, i)),
                pl.BlockSpec((2, block), lambda i, pos: (0, i)),
            ],
            scratch_shapes=[pltpu.VMEM((rows, width), BF16)],
        ),
        out_shape=[
            jax.ShapeDtypeStruct((rows, total), F32),
            jax.ShapeDtypeStruct((2, total), F32),
        ],
        compiler_params=pltpu.CompilerParams(vmem_limit_bytes=VMEM_LIMIT),
        cost_estimate=pl.CostEstimate(
            flops=2 * rows * total * width,
            bytes_accessed=2 * total * width + 4 * rows * total,
            transcendentals=rows * total,
        ),
    )(pos, *unit_arrays, points)


def weigh_body(n_stats, n_e, n_x, pos_ref, *refs):
    stat_refs, refs = refs[:n_stats], refs[n_stats:]
    e_refs, refs = refs[:n_e], refs[n_e:]
    x_refs, refs = refs[:n_x], refs[n_x:]
    mine_ref, theirs_ref, mass_ref, log_ref, scale_ref = refs[:5]
    mass_sums = refs[5:]
    other, chunk = pl.program_id(0), pl.program_id(1)
    width = e_refs[0].shape[1]

    @pl.when(jnp.logical_and(other == 0, chunk == 0))
    def _():
        top = stat_refs[0][0:1, :]
        for ref in stat_refs[1:]:
            top = jnp.maximum(top, ref[0:1, :])
        own = jnp.exp(stat_refs[0][0:1, :] - top)
        total = stat_refs[0][1:2, :] * own
        for ref in stat_refs[1:]:
            total = total + ref[1:2, :] * jnp.exp(ref[0:1, :] - top)
        scale_ref[...] = own / total
        log_ref[...] = top + jnp.log(total)

    @pl.when(chunk == 0)
    def _():
        mine_ref[...] = jnp.zeros_like(mine_ref)
        theirs_ref[...] = jnp.zeros_like(theirs_ref)
        for sums in mass_sums:
            sums[...] = jnp.zeros_like(sums)

    scale = scale_ref[:, pl.ds(pl.multiple_of(chunk * width, width), width)]
    weights = []
    for ref, sums in zip(e_refs, mass_sums):
        rounded = (ref[...] * scale).astype(BF16)
        weights.append(rounded)
        wide = rounded.astype(F32)
        lanes = min(width, 128)
        part = wide[:, :lanes]
        for start in range(lanes, width, lanes):
            part = part + wide[:, start : start + lanes]
        sums[...] += part
    for number, out_ref in enumerate((mine_ref, theirs_ref)):
        out_ref[...] += jnp.dot(
            weights[number % n_e], x_refs[number % n_x][...], preferred_element_type=F32
        )

    @pl.when(chunk == pl.num_programs(1) - 1)
    def _():
        for number, sums in enumerate(mass_sums):
            mass_ref[number : number + 1, :] = jnp.sum(sums[...].T, axis=0, keepdims=True)


def weigh(by_rows, targets, stats, shifted, points, size):
    rows, total = shifted.shape
    width = points.shape[1]
    others = targets.shape[0] // 2
    chunk = divisor(total, 512)
    if by_rows:
        out = (size, width)
        e_specs = [
            pl.BlockSpec((size, chunk), lambda d, k, pos, w=w: (pos[2 * d + w], k)) for w in range(2)
        ]
        x_specs = [pl.BlockSpec((chunk, width), lambda d, k, pos: (k, 0))]
    else:
        out = (rows, size)
        e_specs = [pl.BlockSpec((rows, chunk), lambda d, k, pos: (0, k))]
        x_specs = [
            pl.BlockSpec((chunk, size), lambda d, k, pos, w=w: (k, pos[2 * d + w])) for w in range(2)
        ]
    n_e, n_x = len(e_specs), len(x_specs)
    height = out[0]
    stat_spec = pl.BlockSpec((2, total), lambda d, k, pos: (0, 0), pipeline_mode=pl.Buffered(1))
    return pl.pallas_call(
        functools.partial(weigh_body, len(stats), n_e, n_x),
        grid_spec=pltpu.PrefetchScalarGridSpec(
            num_scalar_prefetch=1,
            grid=(others, total // chunk),
            in_specs=[stat_spec] * len(stats) + e_specs + x_specs,
            out_specs=[
                pl.BlockSpec((None, *out), lambda d, k, pos: (d, 0, 0)),
                pl.BlockSpec((None, *out), lambda d, k, pos: (d, 0, 0)),
                pl.BlockSpec((None, n_e, height), lambda d, k, pos: (d, 0, 0)),
                pl.BlockSpec((1, total), lambda d, k, pos: (0, 0)),
            ],
            scratch_shapes=[pltpu.VMEM((1, total), F32)] + [pltpu.VMEM((height, 128), F32)] * n_e,
        ),
        out_shape=[
            jax.ShapeDtypeStruct((others, *out), F32),
            jax.ShapeDtypeStruct((others, *out), F32),
            jax.ShapeDtypeStruct((others, n_e, height), F32),
            jax.ShapeDtypeStruct((1, total), F32),
        ],
        compiler_params=pltpu.CompilerParams(vmem_limit_bytes=VMEM_LIMIT),
        cost_estimate=pl.CostEstimate(
            flops=4 * others * out[0] * out[1] * total,
            bytes_accessed=others * total * (4 * n_e * height + 2 * n_x * x_specs[0].block_shape[1]),
            transcendentals=0,
        ),
    )(targets, *stats, *[shifted] * n_e, *[points] * n_x)


def finish_body(count, mass_ref, *refs):
    total = refs[0][...]
    for ref in refs[1:count]:
        total = total + ref[...]
    means = total / jnp.maximum(mass_ref[...], 1.0)
    refs[count][...] = normalize_rows(means).astype(BF16)


def finish(mass, terms):
    rows, width = terms[0].shape
    block = divisor(rows, 64)
    spec = pl.BlockSpec((block, width), lambda i: (i, 0))
    return pl.pallas_call(
        functools.partial(finish_body, len(terms)),
        grid=(rows // block,),
        in_specs=[pl.BlockSpec((block, 1), lambda i: (i, 0))] + [spec] * len(terms),
        out_specs=spec,
        out_shape=jax.ShapeDtypeStruct((rows, width), BF16),
        compiler_params=pltpu.CompilerParams(vmem_limit_bytes=VMEM_LIMIT),
        cost_estimate=pl.CostEstimate(
            flops=8 * rows * width, bytes_accessed=4 * rows * width * len(terms), transcendentals=rows
        ),
    )(mass[:, None], *terms)


def on_device(n_pts, n_cen, points, centroids):
    rows, width = centroids.shape
    chips = n_pts // 2
    block = rows // n_pts
    me = lax.axis_index("pts")
    chip, core = me // 2, me % 2

    def to_partner(value):
        return lax.ppermute(value, "pts", [(i, i ^ 1) for i in range(n_pts)])

    def to_chip(value, away):
        moves = [(i, (i + 2 * away) % n_pts) for i in range(n_pts)]
        return lax.ppermute(value, "pts", moves)

    def all_stats(stats):
        found = [stats]
        for away in range(1, n_cen):
            if n_cen & (n_cen - 1):
                moves = [(i, (i + away) % n_cen) for i in range(n_cen)]
            else:
                moves = [(i, i ^ away) for i in range(n_cen)]
            found.append(lax.ppermute(stats, "cen", moves))
        return found

    def blocks_of(aways):
        ids = []
        for away in aways:
            there = (chip + away) % chips
            ids += [2 * there + core, 2 * there + 1 - core]
        return jnp.stack(ids).astype(jnp.int32)

    far = blocks_of(range(1, chips))
    near = blocks_of([0])

    def sums_over_pts(by_rows, stats, shifted, size):
        far_mine, far_theirs, far_mass, logs = weigh(by_rows, far, stats, shifted, points, size)
        far_sums = far_mine + to_partner(far_theirs)
        terms = [to_chip(far_sums[away - 1], away) for away in range(1, chips)]
        near_mine, near_theirs, near_mass, _ = weigh(by_rows, near, stats, shifted, points, size)
        near_terms = [near_mine[0], to_partner(near_theirs)[0]]
        if by_rows:
            mass = jnp.zeros((n_pts, size), F32)
            mass = mass.at[far].set(far_mass.reshape(-1, size)).at[near].set(near_mass.reshape(-1, size))
            mass = lax.psum(mass, "pts")[me]
        else:
            mass = lax.psum(near_mass[0, 0], "pts")
        return near_terms + terms, mass, logs

    pos = jnp.zeros((1,), jnp.int32)
    shifted, stats = scores(fill_from_centroids, pos, [centroids], points, rows)
    for _ in range(ITERS - 1):
        terms, mass, _ = sums_over_pts(True, all_stats(stats), shifted, block)
        mine = finish(mass, terms)
        others = [mine] + [to_chip(mine, away) for away in range(1, chips)]
        units = []
        for unit in others:
            units += [unit, to_partner(unit)]
        order = [near] + [blocks_of([-away]) for away in range(1, chips)]
        shifted, stats = scores(fill_from_blocks, jnp.concatenate(order), units, points, rows)
    terms, mass, logs = sums_over_pts(False, all_stats(stats), shifted, width // n_pts)
    total = terms[0]
    for term in terms[1:]:
        total = total + term
    return (total / jnp.maximum(mass, 1.0)[:, None], logs[0])


def solution(mesh):
    placed = (P("pts", None), P("cen", None))
    return jax.shard_map(
        functools.partial(on_device, mesh.shape["pts"], mesh.shape["cen"]),
        mesh=mesh,
        in_specs=placed,
        out_specs=(P("cen", "pts"), P("pts")),
        check_vma=False,
    )
```

time: 372 us -> 207 us (0.56)
  blocking collectives: 159 us -> 51.4 us
  Pallas kernels: 0 us -> 80.4 us
  matrix products: 69.5 us -> 0 us
  waiting for transfers between devices: 82.1 us -> 22.5 us
  other arithmetic: 40.3 us -> 6.27 us
  starting transfers between devices: 0.3 us -> 28.1 us
  between operations: 13.8 us -> 0.72 us
  local copies, waits for them, and re-layouts: 6.43 us -> 17 us
    pallas_call x0 -> x7, Pallas kernels: none -> 80.4 us  [the longest x4 45.8 us: weigh(): pl.pallas_call(functools.partial(weigh_body, len(stats), n_e, n_x), grid_...]
    pmax x2 -> x0, blocking collectives: 75.9 us -> none  [on_device(): row_max = lax.pmax(local_max, 'cen')]
    dot_general x6 -> x0, matrix products: 69.5 us -> none  [the longest x2 31.9 us: on_device(): lax.dot_general(points, unit_rows, (((1,), (1,)), ((), ())), preferred_el...]
    reduce_scatter x2 -> x0, waiting for transfers between devices: 58 us -> none  [on_device(): shares = lax.psum_scatter(weighted, 'pts', scatter_dimension=1, tiled=True)]
    psum x5 -> x2, blocking collectives: 83.3 us -> 51.4 us  [the longest x1 26.4 us: sums_over_pts(): mass = lax.psum(near_mass[0, 0], 'pts')]
    ppermute x0 -> x23, starting transfers between devices: none -> 28.1 us  [the longest x14 23.6 us: all_stats(): found.append(lax.ppermute(stats, 'cen', moves))]
    all_gather x1 -> x0, waiting for transfers between devices: 24 us -> none  [on_device(): unit_rows = lax.all_gather(unit_shares, 'pts', axis=1, tiled=True)]
    ppermute x0 -> x23, waiting for transfers between devices: none -> 22.5 us  [the longest x3 11.9 us: to_chip(): return lax.ppermute(value, 'pts', moves)]
  transfers between devices with their start and end apart: 3 -> 23, of which waited for: 3 -> 7; matrix products, arithmetic and copies ran while one was open for 4% -> 2% of each run, Pallas kernels for 0% -> 11%
where the time goes in v1:
time: 207 us; the launch traced here: 206 us
  Pallas kernels  80.4 us (39%)
  blocking collectives  51.4 us (25%)
  starting transfers between devices  28.1 us (14%)
  waiting for transfers between devices  22.5 us (11%)
  local copies, waits for them, and re-layouts  17 us (8%)
  other arithmetic  6.27 us (3%)
    pallas_call x4, Pallas kernels, weigh(): pl.pallas_call(functools.partial(weigh_body, len(stats), n_e, n_x), grid_...  45.8 us
    pallas_call x2, Pallas kernels, scores(): pl.pallas_call(functools.partial(score_body, fill, len(unit_arrays), sub)...  32.7 us
    psum x1, blocking collectives, sums_over_pts(): mass = lax.psum(near_mass[0, 0], 'pts')  26.4 us
    psum x1, blocking collectives, sums_over_pts(): mass = lax.psum(mass, 'pts')[me]  25 us
    ppermute x14, starting transfers between devices, all_stats(): found.append(lax.ppermute(stats, 'cen', moves))  23.6 us
    unnamed x10, local copies, waits for them, and re-layouts  15.7 us
    ppermute x3, waiting for transfers between devices, to_chip(): return lax.ppermute(value, 'pts', moves)  11.9 us
    ppermute x14, waiting for transfers between devices, all_stats(): found.append(lax.ppermute(stats, 'cen', moves))  8.74 us
  transfers between devices with their start and end apart: 23, of which 7 were waited for; matrix products, arithmetic and copies ran while one was open for 2% of the time, Pallas kernels for 11%

profile of v1, /device:TPU:0, one launch (start us, length us, event | category | flops | bytes accessed | tf_op | source)
XLA Modules:
  0.0 206.4 jit_solution(12886369478684959607)
XLA Ops:
  0.6 3.4 %copy-done = bf16[4096,1024]{1,0:T(8,128)(2,1)S(1)} copy-done((bf16[4096,1024]{1,0:T(8,128)(2,1)S(1)}, bf16[4096,1024]{1,0:T(8,128)(2,1)}, u32[]{:S(2)}) %copy-start) | copy-done | bytes 8388632
  4.0 2.2 %copy-done.4 = f32[1024,1024]{1,0:T(8,128)S(1)} copy-done((f32[1024,1024]{1,0:T(8,128)S(1)}, f32[1024,1024]{1,0:T(8,128)}, u32[]{:S(2)}) %copy-start.4) | copy-done | bytes 4194328
  6.2 15.7 %shard_map.41 = (f32[1024,4096]{1,0:T(8,128)}, f32[2,4096]{1,0:T(2,128)S(1)}) custom-call(s32[1]{0:T(128)} %constant.52.clone.1.pos_ref, f32[1024,1024]{1,0:T(8,128)S(1)} %copy-done.4, bf16[4096,1024]{1,0:T(8,128)(2,1)S(1)} %copy-done), custom_call_target="tpu_custom_call" | custom-call | flops 8589934592 | bytes 25165824 | tf_op jit(solution)/shard_map/pallas_call | solution.py:69
  21.9 2.9 %collective-permute-start = (f32[2,4096]{1,0:T(2,128)S(1)}, f32[2,4096]{1,0:T(2,128)S(1)}, u32[]{:S(2)}, u32[]{:S(2)}) collective-permute-start(f32[2,4096]{1,0:T(2,128)S(1)} %get-tuple-element.18.refs_0_), channel_id=1, source_target_pairs={{0,1},{1,0},{2,3},{3,2},{4,5},{5,4},{6,7},{7,6},{8,9},{9,8},{10,11... | collective-permute-start | bytes 98312 | tf_op jit(solution)/shard_map/ppermute | solution.py:239
  24.9 1.6 collective-permute-start.1
  26.4 3.0 %collective-permute-start.3 = (f32[2,4096]{1,0:T(2,128)S(1)}, f32[2,4096]{1,0:T(2,128)S(1)}, u32[]{:S(2)}, u32[]{:S(2)}) collective-permute-start(f32[2,4096]{1,0:T(2,128)S(1)} %get-tuple-element.18.refs_0_), channel_id=1, source_target_pairs={{0,4},{1,5},{2,6},{3,7},{4,0},{5,1},{6,2},{7,3},{8,12},{9,13},{10,... | collective-permute-start | bytes 98312 | tf_op jit(solution)/shard_map/ppermute | solution.py:239
  29.4 1.3 collective-permute-start.4
  30.7 3.6 %collective-permute-start.5 = (f32[2,4096]{1,0:T(2,128)S(1)}, f32[2,4096]{1,0:T(2,128)S(1)}, u32[]{:S(2)}, u32[]{:S(2)}) collective-permute-start(f32[2,4096]{1,0:T(2,128)S(1)} %get-tuple-element.18.refs_0_), channel_id=1, source_target_pairs={{0,6},{1,7},{2,4},{3,5},{4,2},{5,3},{6,0},{7,1},{8,14},{9,15},{10,... | collective-permute-start | bytes 98312 | tf_op jit(solution)/shard_map/ppermute | solution.py:239
  34.3 0.0 collective-permute-start.6
  34.4 0.1 pad_add_fusion.2.pos_ref
  34.4 0.9 collective-permute-done.4.refs_5_
  35.4 1.2 collective-permute-done.5.refs_6_
  36.5 4.4 %collective-permute-done.6.refs_7_ = f32[2,4096]{1,0:T(2,128)S(1)} collective-permute-done((f32[2,4096]{1,0:T(2,128)S(1)}, f32[2,4096]{1,0:T(2,128)S(1)}, u32[]{:S(2)}, u32[]{:S(2)}) %collective-permute-start.6) | collective-permute-done | bytes 32800 | tf_op jit(solution)/shard_map/ppermute | solution.py:239
  40.9 3.4 %copy-done.1 = bf16[4096,1024]{1,0:T(8,128)(2,1)S(1)} copy-done((bf16[4096,1024]{1,0:T(8,128)(2,1)S(1)}, bf16[4096,1024]{1,0:T(8,128)(2,1)}, u32[]{:S(2)}) %copy-start.1) | copy-done | bytes 8388632
  44.3 10.6 %shard_map.42 = (f32[1,256,1024]{2,1,0:T(8,128)S(1)}, f32[1,256,1024]{2,1,0:T(8,128)}, f32[1,2,256]{2,1,0:T(2,128)S(1)}, f32[1,4096]{1,0:T(1,128)}) custom-call(s32[2]{0:T(128)S(1)} %pad_add_fusion.2.pos_ref, f32[2,4096]{1,0:T(2,128)S(1)} %get-tuple-element.18.refs_0_, f32[2,4096]{1,0:T(2,128)S(1)} %collective-permute-done.refs_1_, ...), custom_call_target="tpu_custom_call" | custom-call | flops 4294967296 | bytes 16777216 | tf_op jit(solution)/shard_map/pallas_call | solution.py:164
  55.0 0.1 pad_add_fusion.pos_ref
  55.0 3.4 %copy-done.2 = bf16[4096,1024]{1,0:T(8,128)(2,1)S(1)} copy-done((bf16[4096,1024]{1,0:T(8,128)(2,1)S(1)}, bf16[4096,1024]{1,0:T(8,128)(2,1)}, u32[]{:S(2)}) %copy-start.2) | copy-done | bytes 8388632
  58.4 10.7 %shard_map.43 = (f32[1,256,1024]{2,1,0:T(8,128)S(1)}, f32[1,256,1024]{2,1,0:T(8,128)}, f32[1,2,256]{2,1,0:T(2,128)S(1)}, f32[1,4096]{1,0:T(1,128)}) custom-call(s32[2]{0:T(128)S(1)} %pad_add_fusion.pos_ref, f32[2,4096]{1,0:T(2,128)S(1)} %get-tuple-element.18.refs_0_, f32[2,4096]{1,0:T(2,128)S(1)} %collective-permute-done.refs_1_, ...), custom_call_target="tpu_custom_call" | custom-call | flops 4294967296 | bytes 16777216 | tf_op jit(solution)/shard_map/pallas_call | solution.py:164
  69.1 0.5 collective-permute-start.7
  69.6 2.3 %add_bitcast_fusion.1 = f32[256,1024]{1,0:T(8,128)} fusion(f32[1,256,1024]{2,1,0:T(8,128)S(1)} %get-tuple-element.24, f32[1,256,1024]{2,1,0:T(8,128)} %collective-permute-done.8), kind=kLoop, calls=%fused_computation.5 | loop fusion | flops 262144 | bytes 3145728 | tf_op jit(solution)/shard_map/squeeze | solution.py:255
  71.9 1.5 collective-permute-start.9
  73.5 0.1 fusion.6
  73.5 0.1 fusion.7
  73.6 0.6 scatter_custom_fusion
  74.2 0.6 scatter_custom_fusion.1
  74.8 25.0 %psum.14 = f32[4,256]{1,0:T(4,128)S(1)} all-reduce(f32[4,256]{1,0:T(4,128)S(1)} %scatter_custom_fusion.1), channel_id=1, replica_groups=mesh['pts'=4,'cen'=8] {'pts'}, use_global_device_ids=true, to_apply=%region_2.3 | all-reduce | flops 1024 | bytes 8192 | tf_op jit(solution)/shard_map/psum | solution.py:261
  99.8 0.1 copy.4.mass_ref
  100.0 1.9 shard_map.44.refs_0_
  101.9 0.5 collective-permute-start.11
  102.4 11.9 %collective-permute-done.11.refs_2_ = bf16[256,1024]{1,0:T(8,128)(2,1)S(1)} collective-permute-done((bf16[256,1024]{1,0:T(8,128)(2,1)}, bf16[256,1024]{1,0:T(8,128)(2,1)S(1)}, u32[]{:S(2)}, u32[]{:S(2)}) %collective-permute-start.11) | collective-permute-done | bytes 524320 | tf_op jit(solution)/shard_map/ppermute | solution.py:230
  114.3 0.1 pad_add_fusion.1.pos_ref
  114.4 1.8 collective-permute-done.12.refs_3_
  116.2 3.4 %copy-done.3 = bf16[4096,1024]{1,0:T(8,128)(2,1)S(1)} copy-done((bf16[4096,1024]{1,0:T(8,128)(2,1)S(1)}, bf16[4096,1024]{1,0:T(8,128)(2,1)}, u32[]{:S(2)}) %copy-start.3) | copy-done | bytes 8388632
  119.6 17.0 %shard_map.45 = (f32[1024,4096]{1,0:T(8,128)}, f32[2,4096]{1,0:T(2,128)S(1)}) custom-call(s32[4]{0:T(128)S(1)} %pad_add_fusion.1.pos_ref, bf16[256,1024]{1,0:T(8,128)(2,1)} %shard_map.44.refs_0_, bf16[256,1024]{1,0:T(8,128)(2,1)S(1)} %collective-permute-done.10.refs_1_, bf16[256,1024]{1,0:T(8,128)(2,1)S(1)} %collective-permute-done.11.refs_2_, ...), custom_call_target="tpu_custom_call" | custom-call | flops 8589934592 | bytes 25165824 | tf_op jit(solution)/shard_map/pallas_call | solution.py:69
  136.6 0.5 collective-permute-start.13
  137.1 2.9 %collective-permute-start.15 = (f32[2,4096]{1,0:T(2,128)S(1)}, f32[2,4096]{1,0:T(2,128)S(1)}, u32[]{:S(2)}, u32[]{:S(2)}) collective-permute-start(f32[2,4096]{1,0:T(2,128)S(1)} %get-tuple-element.26.refs_0_), channel_id=1, source_target_pairs={{0,3},{1,2},{2,1},{3,0},{4,7},{5,6},{6,5},{7,4},{8,11},{9,10},{10,... | collective-permute-start | bytes 98312 | tf_op jit(solution)/shard_map/ppermute | solution.py:239
  140.1 2.9 %collective-permute-start.17 = (f32[2,4096]{1,0:T(2,128)S(1)}, f32[2,4096]{1,0:T(2,128)S(1)}, u32[]{:S(2)}, u32[]{:S(2)}) collective-permute-start(f32[2,4096]{1,0:T(2,128)S(1)} %get-tuple-element.26.refs_0_), channel_id=1, source_target_pairs={{0,5},{1,4},{2,7},{3,6},{4,1},{5,0},{6,3},{7,2},{8,13},{9,12},{10,... | collective-permute-start | bytes 98312 | tf_op jit(solution)/shard_map/ppermute | solution.py:239
  143.0 0.4 collective-permute-start.18
  143.3 4.4 %collective-permute-start.19 = (f32[2,4096]{1,0:T(2,128)S(1)}, f32[2,4096]{1,0:T(2,128)S(1)}, u32[]{:S(2)}, u32[]{:S(2)}) collective-permute-start(f32[2,4096]{1,0:T(2,128)S(1)} %get-tuple-element.26.refs_0_), channel_id=1, source_target_pairs={{0,7},{1,6},{2,5},{3,4},{4,3},{5,2},{6,1},{7,0},{8,15},{9,14},{10,... | collective-permute-start | bytes 98312 | tf_op jit(solution)/shard_map/ppermute | solution.py:239
  147.7 0.9 collective-permute-done.18.refs_6_
  148.7 1.3 collective-permute-done.19.refs_7_
  150.0 12.2 %shard_map.47 = (f32[1,1024,256]{2,1,0:T(8,128)S(1)}, f32[1,1024,256]{2,1,0:T(8,128)S(1)}, f32[1,1,1024]{2,1,0:T(1,128)}, f32[1,4096]{1,0:T(1,128)}) custom-call(s32[2]{0:T(128)S(1)} %pad_add_fusion.2.pos_ref, f32[2,4096]{1,0:T(2,128)S(1)} %get-tuple-element.26.refs_0_, f32[2,4096]{1,0:T(2,128)S(1)} %collective-permute-done.13.refs_1_, ...), custom_call_target="tpu_custom_call" | custom-call | flops 4294967296 | bytes 20971520 | tf_op jit(solution)/shard_map/pallas_call | solution.py:164
  162.2 12.2 %shard_map.46 = (f32[1,1024,256]{2,1,0:T(8,128)S(1)}, f32[1,1024,256]{2,1,0:T(8,128)S(1)}, f32[1,1,1024]{2,1,0:T(1,128)S(1)}, f32[1,4096]{1,0:T(1,128)}) custom-call(s32[2]{0:T(128)S(1)} %pad_add_fusion.pos_ref, f32[2,4096]{1,0:T(2,128)S(1)} %get-tuple-element.26.refs_0_, f32[2,4096]{1,0:T(2,128)S(1)} %collective-permute-done.13.refs_1_, ...), custom_call_target="tpu_custom_call" | custom-call | flops 4294967296 | bytes 20971520 | tf_op jit(solution)/shard_map/pallas_call | solution.py:164
  174.4 0.5 collective-permute-start.20
  174.9 1.1 add_bitcast_fusion
  176.0 1.5 collective-permute-start.22
  177.6 26.4 %psum.15 = f32[1024]{0:T(1024)S(1)} all-reduce(f32[1024]{0:T(1024)S(1)} %bitcast.36), channel_id=1, replica_groups=mesh['pts'=4,'cen'=8] {'pts'}, use_global_device_ids=true, to_apply=%region_3.4 | all-reduce | flops 1024 | bytes 8192 | tf_op jit(solution)/shard_map/psum | solution.py:263
  203.9 2.5 %fusion = f32[1024,256]{1,0:T(8,128)} fusion(f32[1024,256]{1,0:T(8,128)S(1)} %collective-permute-done.22, f32[1,1024,256]{2,1,0:T(8,128)S(1)} %get-tuple-element.28, f32[1,1024,256]{2,1,0:T(8,128)} %collective-permute-done.20, f32[1024]{0:T(1024)S(1)} %broadcast_maximum_fusion), kind=kLoop, calls=%fused_computation.3 | loop fusion | flops 786432 | bytes 4198400 | tf_op jit(solution)/shard_map/div | solution.py:281
  (30 shorter events, 0.1 us)
Async XLA Ops:
  0.6 3.4 %copy-start = (bf16[4096,1024]{1,0:T(8,128)(2,1)S(1)}, bf16[4096,1024]{1,0:T(8,128)(2,1)}, u32[]{:S(2)}) copy-start(bf16[4096,1024]{1,0:T(8,128)(2,1)} %refs_10_.7) | copy-start | bytes 25165828
  4.0 2.2 %copy-start.4 = (f32[1024,1024]{1,0:T(8,128)S(1)}, f32[1024,1024]{1,0:T(8,128)}, u32[]{:S(2)}) copy-start(f32[1024,1024]{1,0:T(8,128)} %refs_0_.1) | copy-start | bytes 12582916
  21.9 8.8 %collective-permute-start = (f32[2,4096]{1,0:T(2,128)S(1)}, f32[2,4096]{1,0:T(2,128)S(1)}, u32[]{:S(2)}, u32[]{:S(2)}) collective-permute-start(f32[2,4096]{1,0:T(2,128)S(1)} %get-tuple-element.18.refs_0_), channel_id=1, source_target_pairs={{0,1},{1,0},{2,3},{3,2},{4,5},{5,4},{6,7},{7,6},{8,9},{9,8},{10,11... | collective-permute-start | bytes 98312 | tf_op jit(solution)/shard_map/ppermute | solution.py:239
  24.9 9.4 %collective-permute-start.1 = (f32[2,4096]{1,0:T(2,128)S(1)}, f32[2,4096]{1,0:T(2,128)S(1)}, u32[]{:S(2)}, u32[]{:S(2)}) collective-permute-start(f32[2,4096]{1,0:T(2,128)S(1)} %get-tuple-element.18.refs_0_), channel_id=1, source_target_pairs={{0,2},{1,3},{2,0},{3,1},{4,6},{5,7},{6,4},{7,5},{8,10},{9,11},{10,... | collective-permute-start | bytes 98312 | tf_op jit(solution)/shard_map/ppermute | solution.py:239
  26.4 8.0 %collective-permute-start.2 = (f32[2,4096]{1,0:T(2,128)S(1)}, f32[2,4096]{1,0:T(2,128)S(1)}, u32[]{:S(2)}, u32[]{:S(2)}) collective-permute-start(f32[2,4096]{1,0:T(2,128)S(1)} %get-tuple-element.18.refs_0_), channel_id=1, source_target_pairs={{0,3},{1,2},{2,1},{3,0},{4,7},{5,6},{6,5},{7,4},{8,11},{9,10},{10,... | collective-permute-start | bytes 98312 | tf_op jit(solution)/shard_map/ppermute | solution.py:239
  26.4 8.0 %collective-permute-start.3 = (f32[2,4096]{1,0:T(2,128)S(1)}, f32[2,4096]{1,0:T(2,128)S(1)}, u32[]{:S(2)}, u32[]{:S(2)}) collective-permute-start(f32[2,4096]{1,0:T(2,128)S(1)} %get-tuple-element.18.refs_0_), channel_id=1, source_target_pairs={{0,4},{1,5},{2,6},{3,7},{4,0},{5,1},{6,2},{7,3},{8,12},{9,13},{10,... | collective-permute-start | bytes 98312 | tf_op jit(solution)/shard_map/ppermute | solution.py:239
  29.4 5.9 %collective-permute-start.4 = (f32[2,4096]{1,0:T(2,128)S(1)}, f32[2,4096]{1,0:T(2,128)S(1)}, u32[]{:S(2)}, u32[]{:S(2)}) collective-permute-start(f32[2,4096]{1,0:T(2,128)S(1)} %get-tuple-element.18.refs_0_), channel_id=1, source_target_pairs={{0,5},{1,4},{2,7},{3,6},{4,1},{5,0},{6,3},{7,2},{8,13},{9,12},{10,... | collective-permute-start | bytes 98312 | tf_op jit(solution)/shard_map/ppermute | solution.py:239
  30.7 5.8 %collective-permute-start.5 = (f32[2,4096]{1,0:T(2,128)S(1)}, f32[2,4096]{1,0:T(2,128)S(1)}, u32[]{:S(2)}, u32[]{:S(2)}) collective-permute-start(f32[2,4096]{1,0:T(2,128)S(1)} %get-tuple-element.18.refs_0_), channel_id=1, source_target_pairs={{0,6},{1,7},{2,4},{3,5},{4,2},{5,3},{6,0},{7,1},{8,14},{9,15},{10,... | collective-permute-start | bytes 98312 | tf_op jit(solution)/shard_map/ppermute | solution.py:239
  34.3 6.6 %collective-permute-start.6 = (f32[2,4096]{1,0:T(2,128)S(1)}, f32[2,4096]{1,0:T(2,128)S(1)}, u32[]{:S(2)}, u32[]{:S(2)}) collective-permute-start(f32[2,4096]{1,0:T(2,128)S(1)} %get-tuple-element.18.refs_0_), channel_id=1, source_target_pairs={{0,7},{1,6},{2,5},{3,4},{4,3},{5,2},{6,1},{7,0},{8,15},{9,14},{10,... | collective-permute-start | bytes 98312 | tf_op jit(solution)/shard_map/ppermute | solution.py:239
  40.9 3.4 %copy-start.1 = (bf16[4096,1024]{1,0:T(8,128)(2,1)S(1)}, bf16[4096,1024]{1,0:T(8,128)(2,1)}, u32[]{:S(2)}) copy-start(bf16[4096,1024]{1,0:T(8,128)(2,1)} %refs_10_.7) | copy-start | bytes 25165828
  55.0 14.6 %collective-permute-start.8 = (f32[1,256,1024]{2,1,0:T(8,128)}, f32[1,256,1024]{2,1,0:T(8,128)}, u32[]{:S(2)}, u32[]{:S(2)}) collective-permute-start(f32[1,256,1024]{2,1,0:T(8,128)} %get-tuple-element.25), channel_id=1, source_target_pairs={{0,8},{8,0},{16,24},{24,16},{1,9},{9,1},{17,25},{25,17},{2,10},{10... | collective-permute-start | bytes 3145736 | tf_op jit(solution)/shard_map/ppermute | solution.py:226
  55.0 3.4 %copy-start.2 = (bf16[4096,1024]{1,0:T(8,128)(2,1)S(1)}, bf16[4096,1024]{1,0:T(8,128)(2,1)}, u32[]{:S(2)}) copy-start(bf16[4096,1024]{1,0:T(8,128)(2,1)} %refs_10_.7) | copy-start | bytes 25165828
  69.1 30.9 %collective-permute-start.7 = (f32[1,256,1024]{2,1,0:T(8,128)}, f32[1,256,1024]{2,1,0:T(8,128)S(1)}, u32[]{:S(2)}, u32[]{:S(2)}) collective-permute-start(f32[1,256,1024]{2,1,0:T(8,128)} %get-tuple-element.23), channel_id=1, source_target_pairs={{0,8},{8,0},{16,24},{24,16},{1,9},{9,1},{17,25},{25,17},{2,10},{10... | collective-permute-start | bytes 3145736 | tf_op jit(solution)/shard_map/ppermute | solution.py:226
  71.9 28.0 %collective-permute-start.9 = (f32[256,1024]{1,0:T(8,128)}, f32[256,1024]{1,0:T(8,128)S(1)}, u32[]{:S(2)}, u32[]{:S(2)}) collective-permute-start(f32[256,1024]{1,0:T(8,128)} %add_bitcast_fusion.1), channel_id=1, source_target_pairs={{0,16},{8,24},{16,0},{24,8},{1,17},{9,25},{17,1},{25,9},{2,18},{10... | collective-permute-start | bytes 3145736 | tf_op jit(solution)/shard_map/ppermute | solution.py:230
  101.9 12.4 %collective-permute-start.11 = (bf16[256,1024]{1,0:T(8,128)(2,1)}, bf16[256,1024]{1,0:T(8,128)(2,1)S(1)}, u32[]{:S(2)}, u32[]{:S(2)}) collective-permute-start(bf16[256,1024]{1,0:T(8,128)(2,1)} %shard_map.44.refs_0_), channel_id=1, source_target_pairs={{0,16},{8,24},{16,0},{24,8},{1,17},{9,25},{17,1},{25,9},{2,18},{10... | collective-permute-start | bytes 1572872 | tf_op jit(solution)/shard_map/ppermute | solution.py:230
  102.4 12.0 %collective-permute-start.10 = (bf16[256,1024]{1,0:T(8,128)(2,1)}, bf16[256,1024]{1,0:T(8,128)(2,1)S(1)}, u32[]{:S(2)}, u32[]{:S(2)}) collective-permute-start(bf16[256,1024]{1,0:T(8,128)(2,1)} %shard_map.44.refs_0_), channel_id=1, source_target_pairs={{0,8},{8,0},{16,24},{24,16},{1,9},{9,1},{17,25},{25,17},{2,10},{10... | collective-permute-start | bytes 1572872 | tf_op jit(solution)/shard_map/ppermute | solution.py:226
  114.3 1.9 collective-permute-start.12
  116.2 3.4 %copy-start.3 = (bf16[4096,1024]{1,0:T(8,128)(2,1)S(1)}, bf16[4096,1024]{1,0:T(8,128)(2,1)}, u32[]{:S(2)}) copy-start(bf16[4096,1024]{1,0:T(8,128)(2,1)} %refs_10_.7) | copy-start | bytes 25165828
  136.6 6.4 %collective-permute-start.13 = (f32[2,4096]{1,0:T(2,128)S(1)}, f32[2,4096]{1,0:T(2,128)S(1)}, u32[]{:S(2)}, u32[]{:S(2)}) collective-permute-start(f32[2,4096]{1,0:T(2,128)S(1)} %get-tuple-element.26.refs_0_), channel_id=1, source_target_pairs={{0,1},{1,0},{2,3},{3,2},{4,5},{5,4},{6,7},{7,6},{8,9},{9,8},{10,11... | collective-permute-start | bytes 98312 | tf_op jit(solution)/shard_map/ppermute | solution.py:239
  137.1 6.2 %collective-permute-start.14 = (f32[2,4096]{1,0:T(2,128)S(1)}, f32[2,4096]{1,0:T(2,128)S(1)}, u32[]{:S(2)}, u32[]{:S(2)}) collective-permute-start(f32[2,4096]{1,0:T(2,128)S(1)} %get-tuple-element.26.refs_0_), channel_id=1, source_target_pairs={{0,2},{1,3},{2,0},{3,1},{4,6},{5,7},{6,4},{7,5},{8,10},{9,11},{10,... | collective-permute-start | bytes 98312 | tf_op jit(solution)/shard_map/ppermute | solution.py:239
  137.1 10.6 %collective-permute-start.15 = (f32[2,4096]{1,0:T(2,128)S(1)}, f32[2,4096]{1,0:T(2,128)S(1)}, u32[]{:S(2)}, u32[]{:S(2)}) collective-permute-start(f32[2,4096]{1,0:T(2,128)S(1)} %get-tuple-element.26.refs_0_), channel_id=1, source_target_pairs={{0,3},{1,2},{2,1},{3,0},{4,7},{5,6},{6,5},{7,4},{8,11},{9,10},{10,... | collective-permute-start | bytes 98312 | tf_op jit(solution)/shard_map/ppermute | solution.py:239
  140.1 7.7 %collective-permute-start.16 = (f32[2,4096]{1,0:T(2,128)S(1)}, f32[2,4096]{1,0:T(2,128)S(1)}, u32[]{:S(2)}, u32[]{:S(2)}) collective-permute-start(f32[2,4096]{1,0:T(2,128)S(1)} %get-tuple-element.26.refs_0_), channel_id=1, source_target_pairs={{0,4},{1,5},{2,6},{3,7},{4,0},{5,1},{6,2},{7,3},{8,12},{9,13},{10,... | collective-permute-start | bytes 98312 | tf_op jit(solution)/shard_map/ppermute | solution.py:239
  140.1 7.7 %collective-permute-start.17 = (f32[2,4096]{1,0:T(2,128)S(1)}, f32[2,4096]{1,0:T(2,128)S(1)}, u32[]{:S(2)}, u32[]{:S(2)}) collective-permute-start(f32[2,4096]{1,0:T(2,128)S(1)} %get-tuple-element.26.refs_0_), channel_id=1, source_target_pairs={{0,5},{1,4},{2,7},{3,6},{4,1},{5,0},{6,3},{7,2},{8,13},{9,12},{10,... | collective-permute-start | bytes 98312 | tf_op jit(solution)/shard_map/ppermute | solution.py:239
  143.0 5.7 %collective-permute-start.18 = (f32[2,4096]{1,0:T(2,128)S(1)}, f32[2,4096]{1,0:T(2,128)S(1)}, u32[]{:S(2)}, u32[]{:S(2)}) collective-permute-start(f32[2,4096]{1,0:T(2,128)S(1)} %get-tuple-element.26.refs_0_), channel_id=1, source_target_pairs={{0,6},{1,7},{2,4},{3,5},{4,2},{5,3},{6,0},{7,1},{8,14},{9,15},{10,... | collective-permute-start | bytes 98312 | tf_op jit(solution)/shard_map/ppermute | solution.py:239
  143.3 6.6 %collective-permute-start.19 = (f32[2,4096]{1,0:T(2,128)S(1)}, f32[2,4096]{1,0:T(2,128)S(1)}, u32[]{:S(2)}, u32[]{:S(2)}) collective-permute-start(f32[2,4096]{1,0:T(2,128)S(1)} %get-tuple-element.26.refs_0_), channel_id=1, source_target_pairs={{0,7},{1,6},{2,5},{3,4},{4,3},{5,2},{6,1},{7,0},{8,15},{9,14},{10,... | collective-permute-start | bytes 98312 | tf_op jit(solution)/shard_map/ppermute | solution.py:239
  162.2 12.7 %collective-permute-start.21 = (f32[1,1024,256]{2,1,0:T(8,128)S(1)}, f32[1,1024,256]{2,1,0:T(8,128)S(1)}, u32[]{:S(2)}, u32[]{:S(2)}) collective-permute-start(f32[1,1024,256]{2,1,0:T(8,128)S(1)} %get-tuple-element.31), channel_id=1, source_target_pairs={{0,8},{8,0},{16,24},{24,16},{1,9},{9,1},{17,25},{25,17},{2,10},{10... | collective-permute-start | bytes 3145736 | tf_op jit(solution)/shard_map/ppermute | solution.py:226
  174.4 29.5 %collective-permute-start.20 = (f32[1,1024,256]{2,1,0:T(8,128)S(1)}, f32[1,1024,256]{2,1,0:T(8,128)}, u32[]{:S(2)}, u32[]{:S(2)}) collective-permute-start(f32[1,1024,256]{2,1,0:T(8,128)S(1)} %get-tuple-element.29), channel_id=1, source_target_pairs={{0,8},{8,0},{16,24},{24,16},{1,9},{9,1},{17,25},{25,17},{2,10},{10... | collective-permute-start | bytes 3145736 | tf_op jit(solution)/shard_map/ppermute | solution.py:226
  176.0 27.9 %collective-permute-start.22 = (f32[1024,256]{1,0:T(8,128)}, f32[1024,256]{1,0:T(8,128)S(1)}, u32[]{:S(2)}, u32[]{:S(2)}) collective-permute-start(f32[1024,256]{1,0:T(8,128)} %add_bitcast_fusion), channel_id=1, source_target_pairs={{0,16},{8,24},{16,0},{24,8},{1,17},{9,25},{17,1},{25,9},{2,18},{10... | collective-permute-start | bytes 3145736 | tf_op jit(solution)/shard_map/ppermute | solution.py:230

commit v2 on v0

v2 whole, which is shorter than its diff:
```python
import functools

import jax
import jax.numpy as jnp
from jax import lax
from jax.experimental import pallas as pl
from jax.experimental.pallas import tpu as pltpu
from jax.sharding import PartitionSpec as P

ITERS = 2
F32 = jnp.float32
BF16 = jnp.bfloat16
VMEM_LIMIT = 50 * 2**20
LEVELS = 30000.0
LOWEST = -117.0


def divisor(total, wanted):
    size = min(total, wanted)
    while total % size:
        size -= 1
    return size


def round_up(value, unit):
    return -(-value // unit) * unit


def normalize_rows(rows):
    return rows * lax.rsqrt(jnp.sum(rows * rows, axis=1, keepdims=True) + 1e-06)


def params():
    return pltpu.CompilerParams(vmem_limit_bytes=VMEM_LIMIT)


def fetch(x_ref, buffer, semaphores, step, rows, columns=None):
    slot = lax.rem(step, 2)
    source = x_ref.at[rows, :] if columns is None else x_ref.at[rows, columns]
    return pltpu.make_async_copy(source, buffer.at[slot], semaphores.at[slot])


def merge(stats, other):
    top = jnp.maximum(stats[0], other[0])
    return top, stats[1] * jnp.exp(stats[0] - top) + other[1] * jnp.exp(other[0] - top)


def to_column(row, height):
    return jnp.broadcast_to(row, (128, height)).T


def encode(values, scale):
    steps = jnp.floor(jnp.abs(values) * (LEVELS / scale) + 0.5)
    power = jnp.floor(steps * (1.0 / 128.0))
    size = (1.0 + (steps * (1.0 / 128.0) - power)) * jnp.exp2(power + LOWEST)
    return jnp.where(values < 0.0, -size, size).astype(BF16)


def decode(codes, scale):
    wide = codes.astype(F32)
    size = jnp.abs(wide)
    power = jnp.floor(jnp.log2(size))
    steps = 128.0 * (power - LOWEST + (size * jnp.exp2(-power) - 1.0))
    return jnp.where(wide < 0.0, -steps, steps) * (scale * (1.0 / LEVELS))


def fill_from_centroids(pos_ref, unit_refs, units):
    rows = units.shape[0]
    step = divisor(rows, 256)
    for start in range(0, rows, step):
        block = unit_refs[0][start : start + step, :]
        units[start : start + step, :] = normalize_rows(block).astype(BF16)


def fill_from_blocks(pos_ref, unit_refs, units):
    rows = unit_refs[0].shape[0]
    for number, ref in enumerate(unit_refs):
        start = pl.multiple_of(pos_ref[number] * rows, rows)
        units[pl.ds(start, rows), :] = ref[...]


def score_body(fill, count, sub, pos_ref, *refs):
    unit_refs = refs[:count]
    x_ref, e_ref, stat_ref, units, buffer, semaphores = refs[count:]
    step = pl.program_id(0)
    block = buffer.shape[1]

    def points_of(number):
        rows = pl.ds(pl.multiple_of(number * block, block), block)
        return fetch(x_ref, buffer, semaphores, number, rows)

    @pl.when(step == 0)
    def _():
        points_of(0).start()
        fill(pos_ref, unit_refs, units)

    @pl.when(step + 1 < pl.num_programs(0))
    def _():
        points_of(step + 1).start()

    points_of(step).wait()
    slot = lax.rem(step, 2)
    tops, totals = [], []
    for start in range(0, block, sub):
        part = slice(start, start + sub)
        logits = lax.dot_general(
            units[...], buffer[slot, part, :], (((1,), (1,)), ((), ())), preferred_element_type=F32
        )
        top = jnp.max(logits, axis=0, keepdims=True)
        shifted = jnp.exp(logits - top)
        e_ref[:, part] = shifted
        tops.append(top)
        totals.append(jnp.sum(shifted, axis=0, keepdims=True))
    stat_ref[0, pl.ds(step, 1), :] = jnp.concatenate(tops, axis=1)
    stat_ref[1, pl.ds(step, 1), :] = jnp.concatenate(totals, axis=1)


def scores(fill, pos, unit_arrays, points, rows):
    total, width = points.shape
    block = divisor(total, 512)
    sub = divisor(block, 256)
    stat = (2, total // block, block)
    whole = [
        pl.BlockSpec(u.shape, lambda i, pos: (0, 0), pipeline_mode=pl.Buffered(1)) for u in unit_arrays
    ]
    return pl.pallas_call(
        functools.partial(score_body, fill, len(unit_arrays), sub),
        grid_spec=pltpu.PrefetchScalarGridSpec(
            num_scalar_prefetch=1,
            grid=(total // block,),
            in_specs=whole + [pl.BlockSpec(memory_space=pl.ANY)],
            out_specs=[
                pl.BlockSpec((rows, block), lambda i, pos: (0, i)),
                pl.BlockSpec(stat, lambda i, pos: (0, 0, 0)),
            ],
            scratch_shapes=[
                pltpu.VMEM((rows, width), BF16),
                pltpu.VMEM((2, block, width), BF16),
                pltpu.SemaphoreType.DMA((2,)),
            ],
        ),
        out_shape=[
            jax.ShapeDtypeStruct((rows, total), F32),
            jax.ShapeDtypeStruct(stat, F32),
        ],
        compiler_params=params(),
        cost_estimate=pl.CostEstimate(
            flops=2 * rows * total * width,
            bytes_accessed=2 * total * width + 4 * rows * total,
            transcendentals=rows * total,
        ),
    )(pos, *unit_arrays, points)


def weigh_body(by_rows, n_groups, parts, extra, pos_ref, stat_ref, more_ref, *refs):
    top_refs, refs = refs[:n_groups], refs[n_groups:]
    e_refs, refs = refs[:n_groups], refs[n_groups:]
    x_ref, _ = refs[:2]
    out_refs, refs = refs[2 : 2 + parts], refs[2 + parts :]
    scale_refs, refs = refs[:n_groups], refs[n_groups:]
    mass_refs, refs = refs[:n_groups], refs[n_groups:]
    sum_refs, (buffer, semaphores) = refs[:n_groups], refs[n_groups:]
    other, chunk = pl.program_id(0), pl.program_id(1)
    chunks = pl.num_programs(1)
    step = other * chunks + chunk
    height, span = buffer.shape[1:]
    core, chip = pos_ref[0], pos_ref[1]
    pair = e_refs[0].shape[0]
    line = stat_ref.shape[2]
    lines = e_refs[0].shape[1] // line
    chips = n_groups

    def points_of(number):
        rows = pl.ds(pl.multiple_of(lax.rem(number, chunks) * height, height), height)
        if by_rows:
            return fetch(x_ref, buffer, semaphores, number, rows)
        place = pos_ref[2 + lax.div(number, chunks)]
        columns = pl.ds(pl.multiple_of(place * span, span), span)
        return fetch(x_ref, buffer, semaphores, number, rows, columns)

    @pl.when(step == 0)
    def _():
        points_of(0).start()
        top, total = merge(stat_ref, more_ref)
        for ref, scale_ref in zip(top_refs, scale_refs):
            scale_ref[...] = jnp.exp(ref[0] - top) / total

    @pl.when(step + 1 < pl.num_programs(0) * chunks)
    def _():
        points_of(step + 1).start()

    points_of(step).wait()
    slot = lax.rem(step, 2)

    @pl.when(chunk == 0)
    def _():
        for ref in (*mass_refs, *sum_refs):
            ref[...] = jnp.zeros_like(ref)

    for e_ref, scale_ref, mass_ref, sum_ref in zip(e_refs, scale_refs, mass_refs, sum_refs):
        rounded = []
        mass = mass_ref[...]
        for number in range(lines):
            scale = scale_ref[pl.ds(chunk * lines + number, 1), :]
            weights = (e_ref[:, number * line : (number + 1) * line] * scale).astype(BF16)
            rounded.append(weights)
            wide = weights.astype(F32)
            lanes = min(line, 128)
            for start in range(0, line, lanes):
                mass = mass + wide[:, start : start + lanes]
        mass_ref[...] = mass
        weights = jnp.concatenate(rounded, axis=1) if lines > 1 else rounded[0]
        sum_ref[...] += jnp.dot(weights, buffer[slot], preferred_element_type=F32)

    @pl.when(chunk == chunks - 1)
    def _():
        rows = out_refs[0].shape[0] - extra
        width = out_refs[0].shape[1]
        masses = [jnp.sum(ref[...].T, axis=0, keepdims=True) for ref in mass_refs]
        for part, ref in enumerate(out_refs):
            place = lax.rem(core + part, parts)
            ref[rows:, :] = jnp.zeros((extra, width), F32)
            if by_rows:
                start = pl.multiple_of(place * rows, rows)
                ref[:rows, :] = sum_refs[0][pl.ds(start, rows), :] if parts > 1 else sum_refs[0][...]
                mass = masses[0]
                if parts > 1:
                    mass = jnp.where(place == 0, mass[:, :rows], mass[:, rows:])
                ref[rows : rows + 1, :rows] = mass
                continue
            for group, (sum_ref, mass) in enumerate(zip(sum_refs, masses)):
                owner = lax.rem(chip + group, chips)
                sums = sum_ref[...]
                if parts > 1:
                    sums = jnp.where(place == 0, sums[:, :width], sums[:, width:])
                ref[pl.ds(pl.multiple_of(owner * pair, pair), pair), :] = sums
                for number in range(pair // width):
                    ref[pl.ds(rows + owner * (pair // width) + number, 1), :] = mass[
                        :, number * width : (number + 1) * width
                    ]


def weigh(by_rows, parts, pos, stats, tops, shifted, pair, points, after):
    total, width = points.shape
    others = pos.shape[0] - 2
    cores = 2
    line = stats[0].shape[2]
    chunk = line * divisor(total // line, 2)
    if by_rows:
        rows, cols = pair // cores, width
        height = rows * parts
        sums = (height, width)
        e_specs = [pl.BlockSpec((height, chunk), lambda d, k, pos: (pos[2 + d], k))]
    else:
        rows = sum(e.shape[0] for e in shifted)
        cols = width * pair // (cores * rows)
        height = pair
        sums = (pair, cols * parts)
        e_specs, e_args = [], []
        for e in shifted:
            for number in range(e.shape[0] // pair):
                e_specs.append(pl.BlockSpec((pair, chunk), lambda d, k, pos, n=number: (n, k)))
                e_args.append(e)
        tops = [top for top, e in zip(tops, shifted) for _ in range(e.shape[0] // pair)]
        shifted = e_args
    n_groups = len(e_specs)
    extra = round_up(-(-rows // cols), 8)
    out = (rows + extra, cols)
    stat_spec = pl.BlockSpec(stats[0].shape, lambda d, k, pos: (0, 0, 0))
    out_spec = pl.BlockSpec((None, *out), lambda d, k, pos: (d, 0, 0))
    out_shape = jax.ShapeDtypeStruct((others, *out), F32)
    return pl.pallas_call(
        functools.partial(weigh_body, by_rows, n_groups, parts, extra),
        grid_spec=pltpu.PrefetchScalarGridSpec(
            num_scalar_prefetch=1,
            grid=(others, total // chunk),
            in_specs=[stat_spec] * (2 + n_groups) + e_specs + [pl.BlockSpec(memory_space=pl.ANY)] * 2,
            out_specs=[out_spec] * parts,
            scratch_shapes=[pltpu.VMEM(stats[0].shape[1:], F32)] * n_groups
            + [pltpu.VMEM((height, 128), F32)] * n_groups
            + [pltpu.VMEM(sums, F32)] * n_groups
            + [pltpu.VMEM((2, chunk, sums[1]), BF16), pltpu.SemaphoreType.DMA((2,))],
        ),
        out_shape=[out_shape] * parts,
        compiler_params=params(),
        cost_estimate=pl.CostEstimate(
            flops=2 * others * n_groups * sums[0] * sums[1] * total,
            bytes_accessed=others * total * (4 * n_groups * height + 2 * sums[1]),
            transcendentals=0,
        ),
    )(pos, *stats, *tops, *shifted, points, after)


def fold_body(rows, lines, mine_ref, theirs_ref, after_ref, out_ref):
    width = out_ref.shape[1]
    step = divisor(rows, 128) if lines == 1 else width
    out_ref[rows:, :] = jnp.zeros((out_ref.shape[0] - rows, width), BF16)
    scales = []
    for start in range(0, rows, step):
        part = slice(start, start + step)
        total = mine_ref[part, :] + theirs_ref[part, :]
        top = jnp.max(jnp.abs(total), axis=1, keepdims=True)
        scale = jnp.maximum(top * 1.01, 1e-30).astype(BF16)
        out_ref[part, :] = encode(total, scale.astype(F32))
        scales.append(jnp.broadcast_to(scale.astype(F32), (step, 128)).T[0:1, :])
    mass = mine_ref[rows : rows + lines, :] + theirs_ref[rows : rows + lines, :]
    if lines == 1:
        out_ref[rows : rows + 1, :rows] = jnp.concatenate(scales, axis=1).astype(BF16)
    else:
        out_ref[rows : rows + lines, :] = jnp.concatenate(scales, axis=0).astype(BF16)
    for number in range(1, 4):
        rounded = mass.astype(BF16)
        out_ref[rows + number * lines : rows + (number + 1) * lines, :] = rounded
        mass = mass - rounded.astype(F32)


def fold(mine, theirs, after):
    others, height, width = mine.shape
    return pl.pallas_call(
        functools.partial(fold_body, *shape_of(height, width)),
        grid=(others,),
        in_specs=[pl.BlockSpec((None, height, width), lambda d: (d, 0, 0))] * 2
        + [pl.BlockSpec(memory_space=pl.ANY)],
        out_specs=pl.BlockSpec((None, coded_height(height, width), width), lambda d: (d, 0, 0)),
        out_shape=jax.ShapeDtypeStruct((others, coded_height(height, width), width), BF16),
        compiler_params=params(),
        cost_estimate=pl.CostEstimate(
            flops=20 * others * height * width,
            bytes_accessed=10 * others * height * width,
            transcendentals=others * height * width,
        ),
    )(mine, theirs, after)


def shape_of(height, width):
    rows = height - 8
    while rows + round_up(-(-rows // width), 8) != height:
        rows -= 8
    return rows, -(-rows // width)


def coded_height(height, width):
    rows, lines = shape_of(height, width)
    return rows + round_up(4 * lines, 16)


def finish_body(rows, lines, as_units, mine_ref, theirs_ref, *refs):
    code_refs, out_ref = refs[:-1], refs[-1]
    width = out_ref.shape[1]
    step = divisor(rows, 128) if lines == 1 else width
    mass = mine_ref[rows : rows + lines, :] + theirs_ref[rows : rows + lines, :]
    for ref in code_refs:
        for number in range(1, 4):
            start = rows + number * lines
            mass = mass + ref[start : start + lines, :].astype(F32)

    def column(values, number):
        if lines == 1:
            line = values[:, number * step : (number + 1) * step]
        else:
            line = values[number : number + 1, :]
        return to_column(line, step)[:, 0:1]

    scales = [ref[rows : rows + lines, :].astype(F32) for ref in code_refs]
    for number in range(rows // step):
        part = slice(number * step, (number + 1) * step)
        total = mine_ref[part, :] + theirs_ref[part, :]
        for ref, scale in zip(code_refs, scales):
            total = total + decode(ref[part, :], column(scale, number))
        means = total / jnp.maximum(column(mass, number), 1.0)
        out_ref[part, :] = normalize_rows(means).astype(BF16) if as_units else means


def finish(as_units, mine, theirs, codes):
    height, width = mine.shape
    rows, lines = shape_of(height, width)
    out_type = BF16 if as_units else F32
    return pl.pallas_call(
        functools.partial(finish_body, rows, lines, as_units),
        out_shape=jax.ShapeDtypeStruct((rows, width), out_type),
        compiler_params=params(),
        cost_estimate=pl.CostEstimate(
            flops=30 * rows * width,
            bytes_accessed=(12 + 2 * len(codes)) * rows * width,
            transcendentals=2 * rows * width,
        ),
    )(mine, theirs, *codes)


def merge_body(one_ref, two_ref, out_ref):
    out_ref[0], out_ref[1] = merge(one_ref, two_ref)


def merged(one, two):
    return pl.pallas_call(
        merge_body, out_shape=jax.ShapeDtypeStruct(one.shape, F32), compiler_params=params()
    )(one, two)


def log_body(one_ref, two_ref, out_ref):
    top, total = merge(one_ref, two_ref)
    out_ref[...] = top + jnp.log(total)


def log_norms(one, two):
    return pl.pallas_call(
        log_body, out_shape=jax.ShapeDtypeStruct(one.shape[1:], F32), compiler_params=params()
    )(one, two).reshape(-1)


def on_device(n_pts, n_cen, points, centroids):
    rows, width = centroids.shape
    cores = 2
    chips = n_pts // cores
    pair = rows // chips
    me = lax.axis_index("pts")
    chip, core = lax.div(me, cores), lax.rem(me, cores)

    def to_partner(value):
        return lax.ppermute(value, "pts", [(i, i ^ 1) for i in range(n_pts)])

    def to_chip(value, away):
        moves = [(i, (i + cores * away) % n_pts) for i in range(n_pts)]
        return lax.ppermute(value, "pts", moves)

    def over_centroids(stats):
        if n_cen & (n_cen - 1):
            found = [stats]
            for away in range(1, n_cen):
                moves = [(i, (i + away) % n_cen) for i in range(n_cen)]
                found.append(lax.ppermute(stats, "cen", moves))
            return functools.reduce(merged, found[:-1]), found[-1]
        away = 1
        while True:
            moves = [(i, i ^ away) for i in range(n_cen)]
            other = lax.ppermute(stats, "cen", moves)
            away *= 2
            if away >= n_cen:
                return stats, other
            stats = merged(stats, other)

    def places(blocks):
        return jnp.stack([core, chip, *blocks]).astype(jnp.int32)

    far = places([lax.rem(chip + away, chips) for away in range(1, chips)])
    own_block, partner_block = places([me]), places([cores * chip + 1 - core])

    def sums_over_pts(by_rows, stats, tops, shifted):
        def weighted(parts, pos, after):
            return weigh(by_rows, parts, pos, stats, tops, shifted, pair, points, after)

        far_mine, far_theirs = weighted(cores, far, stats[0])
        far_found = to_partner(far_theirs)
        (near_theirs,) = weighted(1, partner_block, far_theirs)
        near_found = to_partner(near_theirs)
        coded = fold(far_mine, far_found, near_theirs)
        codes = [to_chip(coded[away - 1], away) for away in range(1, chips)]
        (near_mine,) = weighted(1, own_block, coded)
        return finish(by_rows, near_mine[0], near_found[0], codes)

    here = jnp.zeros((1,), jnp.int32)
    shifted, own = scores(fill_from_centroids, here, [centroids], points, rows)
    stats = over_centroids(own)
    tops, shifted = [own], [shifted]
    for _ in range(ITERS - 1):
        mine = sums_over_pts(True, stats, tops, shifted)
        away_units = [to_chip(mine, -away) for away in range(1, chips)]
        order = jnp.stack([core, 1 - core]).astype(jnp.int32)
        near_e, near_own = scores(fill_from_blocks, order, [mine, to_partner(mine)], points, pair)
        blocks = [unit for mine in away_units for unit in (mine, to_partner(mine))]
        order = jnp.stack([cores * i + place for i in range(chips - 1) for place in (core, 1 - core)])
        far_e, far_own = scores(
            fill_from_blocks, order.astype(jnp.int32), blocks, points, rows - pair
        )
        tops, shifted = [near_own, far_own], [near_e, far_e]
        stats = over_centroids(merged(near_own, far_own))
    means = sums_over_pts(False, stats, tops, shifted)
    return (means, log_norms(*stats))


def solution(mesh):
    placed = (P("pts", None), P("cen", None))
    return jax.shard_map(
        functools.partial(on_device, mesh.shape["pts"], mesh.shape["cen"]),
        mesh=mesh,
        in_specs=placed,
        out_specs=(P("cen", "pts"), P("pts")),
        check_vma=False,
    )
```

time: 372 us -> 161 us (0.43)
  blocking collectives: 159 us -> 0 us
  Pallas kernels: 0 us -> 107 us
  matrix products: 69.5 us -> 0 us
  waiting for transfers between devices: 82.1 us -> 30.1 us
  other arithmetic: 40.3 us -> 0.23 us
  starting transfers between devices: 0.3 us -> 21.1 us
  between operations: 13.8 us -> 0.79 us
  local copies, waits for them, and re-layouts: 6.43 us -> 0.61 us
    pallas_call x0 -> x19, Pallas kernels: none -> 107 us  [the longest x6 58.6 us: weigh(): pl.pallas_call(functools.partial(weigh_body, by_rows, n_groups, parts, ex...]
    psum x5 -> x0, blocking collectives: 83.3 us -> none  [the longest x2 66.2 us: on_device(): row_total = lax.psum(jnp.sum(shifted, axis=1), 'cen')]
    pmax x2 -> x0, blocking collectives: 75.9 us -> none  [on_device(): row_max = lax.pmax(local_max, 'cen')]
    dot_general x6 -> x0, matrix products: 69.5 us -> none  [the longest x2 31.9 us: on_device(): lax.dot_general(points, unit_rows, (((1,), (1,)), ((), ())), preferred_el...]
    reduce_scatter x2 -> x0, waiting for transfers between devices: 58 us -> none  [on_device(): shares = lax.psum_scatter(weighted, 'pts', scatter_dimension=1, tiled=True)]
    ppermute x0 -> x15, waiting for transfers between devices: none -> 30.1 us  [the longest x3 17.8 us: to_chip(): return lax.ppermute(value, 'pts', moves)]
    all_gather x1 -> x0, waiting for transfers between devices: 24 us -> none  [on_device(): unit_rows = lax.all_gather(unit_shares, 'pts', axis=1, tiled=True)]
    ppermute x0 -> x15, starting transfers between devices: none -> 21.1 us  [the longest x6 14.4 us: over_centroids(): other = lax.ppermute(stats, 'cen', moves)]
  transfers between devices with their start and end apart: 3 -> 15, of which waited for: 3 -> 9; matrix products, arithmetic and copies ran while one was open for 4% -> 1% of each run, Pallas kernels for 0% -> 32%
where the time goes in v2:
time: 161 us; the launch traced here: 160 us
  Pallas kernels  107 us (66%)
  waiting for transfers between devices  30.1 us (19%)
  starting transfers between devices  21.1 us (13%)
    pallas_call x6, Pallas kernels, weigh(): pl.pallas_call(functools.partial(weigh_body, by_rows, n_groups, parts, ex...  58.6 us
    pallas_call x3, Pallas kernels, scores(): pl.pallas_call(functools.partial(score_body, fill, len(unit_arrays), sub)...  44.2 us
    ppermute x3, waiting for transfers between devices, to_chip(): return lax.ppermute(value, 'pts', moves)  17.8 us
    ppermute x6, starting transfers between devices, over_centroids(): other = lax.ppermute(stats, 'cen', moves)  14.4 us
    ppermute x6, waiting for transfers between devices, over_centroids(): other = lax.ppermute(stats, 'cen', moves)  12.3 us
    ppermute x3, starting transfers between devices, to_chip(): return lax.ppermute(value, 'pts', moves)  5.39 us
  transfers between devices with their start and end apart: 15, of which 9 were waited for; matrix products, arithmetic and copies ran while one was open for 1% of the time, Pallas kernels for 32%

profile of v2, /device:TPU:0, one launch (start us, length us, event | category | flops | bytes accessed | tf_op | source)
XLA Modules:
  0.0 160.1 jit_solution(5832056143091079375)
XLA Ops:
  0.6 19.0 %shard_map.41 = (f32[1024,4096]{1,0:T(8,128)}, f32[2,8,512]{2,1,0:T(8,128)S(1)}) custom-call(s32[1]{0:T(128)} %constant.16.clone.1.pos_ref, f32[1024,1024]{1,0:T(8,128)} %refs_0_.1, bf16[4096,1024]{1,0:T(8,128)(2,1)} %refs_4_.5), custom_call_target="tpu_custom_call" | custom-call | flops 8589934592 | bytes 25165824 | tf_op jit(solution)/shard_map/pallas_call | solution.py:126
  19.6 3.0 %collective-permute-start = (f32[2,8,512]{2,1,0:T(8,128)S(1)}, f32[2,8,512]{2,1,0:T(8,128)S(1)}, u32[]{:S(2)}, u32[]{:S(2)}) collective-permute-start(f32[2,8,512]{2,1,0:T(8,128)S(1)} %get-tuple-element.12.one_ref.refs_0_), channel_id=1, source_target_pairs={{0,1},{1,0},{2,3},{3,2},{4,5},{5,4},{6,7},{7,6},{8,9},{9,8},{10,11... | collective-permute-start | bytes 98312 | tf_op jit(solution)/shard_map/ppermute | solution.py:436
  22.6 1.9 %collective-permute-done.two_ref = f32[2,8,512]{2,1,0:T(8,128)S(1)} collective-permute-done((f32[2,8,512]{2,1,0:T(8,128)S(1)}, f32[2,8,512]{2,1,0:T(8,128)S(1)}, u32[]{:S(2)}, u32[]{:S(2)}) %collective-permute-start) | collective-permute-done | bytes 32800 | tf_op jit(solution)/shard_map/ppermute | solution.py:436
  24.5 2.2 %collective-permute-start.1 = (f32[2,8,512]{2,1,0:T(8,128)S(1)}, f32[2,8,512]{2,1,0:T(8,128)S(1)}, u32[]{:S(2)}, u32[]{:S(2)}) collective-permute-start(f32[2,8,512]{2,1,0:T(8,128)S(1)} %shard_map.42.one_ref), channel_id=1, source_target_pairs={{0,2},{1,3},{2,0},{3,1},{4,6},{5,7},{6,4},{7,5},{8,10},{9,11},{10,... | collective-permute-start | bytes 98312 | tf_op jit(solution)/shard_map/ppermute | solution.py:436
  26.7 1.9 %collective-permute-done.1.two_ref = f32[2,8,512]{2,1,0:T(8,128)S(1)} collective-permute-done((f32[2,8,512]{2,1,0:T(8,128)S(1)}, f32[2,8,512]{2,1,0:T(8,128)S(1)}, u32[]{:S(2)}, u32[]{:S(2)}) %collective-permute-start.1) | collective-permute-done | bytes 32800 | tf_op jit(solution)/shard_map/ppermute | solution.py:436
  28.6 3.1 %collective-permute-start.2 = (f32[2,8,512]{2,1,0:T(8,128)S(1)}, f32[2,8,512]{2,1,0:T(8,128)S(1)}, u32[]{:S(2)}, u32[]{:S(2)}) collective-permute-start(f32[2,8,512]{2,1,0:T(8,128)S(1)} %shard_map.43.stat_ref.refs_3_), channel_id=1, source_target_pairs={{0,4},{1,5},{2,6},{3,7},{4,0},{5,1},{6,2},{7,3},{8,12},{9,13},{10,... | collective-permute-start | bytes 98312 | tf_op jit(solution)/shard_map/ppermute | solution.py:436
  31.7 0.1 pad_add_fusion.3.pos_ref
  31.8 1.8 %collective-permute-done.2.more_ref = f32[2,8,512]{2,1,0:T(8,128)S(1)} collective-permute-done((f32[2,8,512]{2,1,0:T(8,128)S(1)}, f32[2,8,512]{2,1,0:T(8,128)S(1)}, u32[]{:S(2)}, u32[]{:S(2)}) %collective-permute-start.2) | collective-permute-done | bytes 32800 | tf_op jit(solution)/shard_map/ppermute | solution.py:436
  33.6 10.4 %shard_map.44 = (f32[1,264,1024]{2,1,0:T(8,128)S(1)}, f32[1,264,1024]{2,1,0:T(8,128)S(1)}) custom-call(s32[3]{0:T(128)S(1)} %pad_add_fusion.3.pos_ref, f32[2,8,512]{2,1,0:T(8,128)S(1)} %shard_map.43.stat_ref.refs_3_, f32[2,8,512]{2,1,0:T(8,128)S(1)} %collective-permute-done.2.more_ref, f32[2,8,512]{2,1,0:T(8,128)S(1)} %get-tuple-element.12.one_ref.refs_0_, ...), custom_call_target="tpu_custom_call" | custom-call | flops 4294967296 | bytes 16777216 | tf_op jit(solution)/shard_map/pallas_call | solution.py:272
  44.0 0.1 collective-permute-start.3
  44.1 0.1 pad_add_fusion
  44.2 8.1 %shard_map.45.after_ref = f32[1,264,1024]{2,1,0:T(8,128)S(1)} custom-call(s32[3]{0:T(128)S(1)} %get-tuple-element.23.pos_ref, f32[2,8,512]{2,1,0:T(8,128)S(1)} %shard_map.43.stat_ref.refs_3_, f32[2,8,512]{2,1,0:T(8,128)S(1)} %collective-permute-done.2.more_ref, f32[2,8,512]{2,1,0:T(8,128)S(1)} %get-tuple-element.12.one_ref.refs_0_, ...), custom_call_target="tpu_custom_call" | custom-call | flops 2147483648 | bytes 12582912 | tf_op jit(solution)/shard_map/pallas_call | solution.py:272
  52.4 0.6 collective-permute-start.4
  52.9 0.0 collective-permute-done.3.theirs_ref
  52.9 0.7 shard_map.46.refs_3_
  53.6 1.9 %collective-permute-start.5 = (bf16[272,1024]{1,0:T(8,128)(2,1)S(1)}, bf16[272,1024]{1,0:T(8,128)(2,1)S(1)}, u32[]{:S(2)}, u32[]{:S(2)}) collective-permute-start(bf16[272,1024]{1,0:T(8,128)(2,1)S(1)} %bitcast.16), channel_id=1, source_target_pairs={{0,16},{8,24},{16,0},{24,8},{1,17},{9,25},{17,1},{25,9},{2,18},{10... | collective-permute-start | bytes 1671176 | tf_op jit(solution)/shard_map/ppermute | solution.py:424
  55.5 8.1 %shard_map.47 = f32[1,264,1024]{2,1,0:T(8,128)S(1)} custom-call(s32[3]{0:T(128)S(1)} %get-tuple-element.22.pos_ref, f32[2,8,512]{2,1,0:T(8,128)S(1)} %shard_map.43.stat_ref.refs_3_, f32[2,8,512]{2,1,0:T(8,128)S(1)} %collective-permute-done.2.more_ref, f32[2,8,512]{2,1,0:T(8,128)S(1)} %get-tuple-element.12.one_ref.refs_0_, ...), custom_call_target="tpu_custom_call" | custom-call | flops 2147483648 | bytes 12582912 | tf_op jit(solution)/shard_map/pallas_call | solution.py:272
  63.7 0.0 collective-permute-done.4
  63.7 4.7 %collective-permute-done.5.refs_0_ = bf16[272,1024]{1,0:T(8,128)(2,1)S(1)} collective-permute-done((bf16[272,1024]{1,0:T(8,128)(2,1)S(1)}, bf16[272,1024]{1,0:T(8,128)(2,1)S(1)}, u32[]{:S(2)}, u32[]{:S(2)}) %collective-permute-start.5) | collective-permute-done | bytes 557088 | tf_op jit(solution)/shard_map/ppermute | solution.py:424
  68.3 0.9 shard_map.48.refs_0_
  69.3 1.8 %collective-permute-start.7 = (bf16[256,1024]{1,0:T(8,128)(2,1)S(1)}, bf16[256,1024]{1,0:T(8,128)(2,1)S(1)}, u32[]{:S(2)}, u32[]{:S(2)}) collective-permute-start(bf16[256,1024]{1,0:T(8,128)(2,1)S(1)} %shard_map.48.refs_0_), channel_id=1, source_target_pairs={{0,16},{8,24},{16,0},{24,8},{1,17},{9,25},{17,1},{25,9},{2,18},{10... | collective-permute-start | bytes 1572872 | tf_op jit(solution)/shard_map/ppermute | solution.py:424
  71.1 0.0 collective-permute-start.6
  71.1 11.4 %collective-permute-done.7.refs_0_ = bf16[256,1024]{1,0:T(8,128)(2,1)S(1)} collective-permute-done((bf16[256,1024]{1,0:T(8,128)(2,1)S(1)}, bf16[256,1024]{1,0:T(8,128)(2,1)S(1)}, u32[]{:S(2)}, u32[]{:S(2)}) %collective-permute-start.7) | collective-permute-done | bytes 524320 | tf_op jit(solution)/shard_map/ppermute | solution.py:424
  82.5 0.0 collective-permute-start.8
  82.5 0.1 pad_add_fusion.2.pos_ref
  82.6 0.0 collective-permute-done.6.refs_1_
  82.6 12.6 %shard_map.49 = (f32[512,4096]{1,0:T(8,128)}, f32[2,8,512]{2,1,0:T(8,128)S(1)}) custom-call(s32[2]{0:T(128)S(1)} %pad_add_fusion.2.pos_ref, bf16[256,1024]{1,0:T(8,128)(2,1)S(1)} %shard_map.48.refs_0_, bf16[256,1024]{1,0:T(8,128)(2,1)S(1)} %collective-permute-done.6.refs_1_, bf16[4096,1024]{1,0:T(8,128)(2,1)} %refs_4_.5), custom_call_target="tpu_custom_call" | custom-call | flops 4294967296 | bytes 16777216 | tf_op jit(solution)/shard_map/pallas_call | solution.py:126
  95.2 0.0 collective-permute-done.8.refs_1_
  95.2 12.6 %shard_map.50 = (f32[512,4096]{1,0:T(8,128)}, f32[2,8,512]{2,1,0:T(8,128)S(1)}) custom-call(s32[2]{0:T(128)S(1)} %pad_add_fusion.2.pos_ref, bf16[256,1024]{1,0:T(8,128)(2,1)S(1)} %collective-permute-done.7.refs_0_, bf16[256,1024]{1,0:T(8,128)(2,1)S(1)} %collective-permute-done.8.refs_1_, bf16[4096,1024]{1,0:T(8,128)(2,1)} %refs_4_.5), custom_call_target="tpu_custom_call" | custom-call | flops 4294967296 | bytes 16777216 | tf_op jit(solution)/shard_map/pallas_call | solution.py:126
  107.8 1.7 %collective-permute-start.9 = (f32[2,8,512]{2,1,0:T(8,128)S(1)}, f32[2,8,512]{2,1,0:T(8,128)S(1)}, u32[]{:S(2)}, u32[]{:S(2)}) collective-permute-start(f32[2,8,512]{2,1,0:T(8,128)S(1)} %shard_map.51.one_ref), channel_id=1, source_target_pairs={{0,1},{1,0},{2,3},{3,2},{4,5},{5,4},{6,7},{7,6},{8,9},{9,8},{10,11... | collective-permute-start | bytes 98312 | tf_op jit(solution)/shard_map/ppermute | solution.py:436
  109.5 2.3 %collective-permute-done.9.two_ref = f32[2,8,512]{2,1,0:T(8,128)S(1)} collective-permute-done((f32[2,8,512]{2,1,0:T(8,128)S(1)}, f32[2,8,512]{2,1,0:T(8,128)S(1)}, u32[]{:S(2)}, u32[]{:S(2)}) %collective-permute-start.9) | collective-permute-done | bytes 32800 | tf_op jit(solution)/shard_map/ppermute | solution.py:436
  111.8 1.7 %collective-permute-start.10 = (f32[2,8,512]{2,1,0:T(8,128)S(1)}, f32[2,8,512]{2,1,0:T(8,128)S(1)}, u32[]{:S(2)}, u32[]{:S(2)}) collective-permute-start(f32[2,8,512]{2,1,0:T(8,128)S(1)} %shard_map.52.one_ref), channel_id=1, source_target_pairs={{0,2},{1,3},{2,0},{3,1},{4,6},{5,7},{6,4},{7,5},{8,10},{9,11},{10,... | collective-permute-start | bytes 98312 | tf_op jit(solution)/shard_map/ppermute | solution.py:436
  113.6 2.2 %collective-permute-done.10.two_ref = f32[2,8,512]{2,1,0:T(8,128)S(1)} collective-permute-done((f32[2,8,512]{2,1,0:T(8,128)S(1)}, f32[2,8,512]{2,1,0:T(8,128)S(1)}, u32[]{:S(2)}, u32[]{:S(2)}) %collective-permute-start.10) | collective-permute-done | bytes 32800 | tf_op jit(solution)/shard_map/ppermute | solution.py:436
  115.8 2.8 %collective-permute-start.11 = (f32[2,8,512]{2,1,0:T(8,128)S(1)}, f32[2,8,512]{2,1,0:T(8,128)S(1)}, u32[]{:S(2)}, u32[]{:S(2)}) collective-permute-start(f32[2,8,512]{2,1,0:T(8,128)S(1)} %shard_map.53.stat_ref.refs_5_.one_ref), channel_id=1, source_target_pairs={{0,4},{1,5},{2,6},{3,7},{4,0},{5,1},{6,2},{7,3},{8,12},{9,13},{10,... | collective-permute-start | bytes 98312 | tf_op jit(solution)/shard_map/ppermute | solution.py:436
  118.6 2.1 %collective-permute-done.11.more_ref.two_ref = f32[2,8,512]{2,1,0:T(8,128)S(1)} collective-permute-done((f32[2,8,512]{2,1,0:T(8,128)S(1)}, f32[2,8,512]{2,1,0:T(8,128)S(1)}, u32[]{:S(2)}, u32[]{:S(2)}) %collective-permute-start.11) | collective-permute-done | bytes 32800 | tf_op jit(solution)/shard_map/ppermute | solution.py:436
  120.7 11.7 %shard_map.54 = (f32[1,1032,256]{2,1,0:T(8,128)S(1)}, f32[1,1032,256]{2,1,0:T(8,128)S(1)}) custom-call(s32[3]{0:T(128)S(1)} %pad_add_fusion.3.pos_ref, f32[2,8,512]{2,1,0:T(8,128)S(1)} %shard_map.53.stat_ref.refs_5_.one_ref, f32[2,8,512]{2,1,0:T(8,128)S(1)} %collective-permute-done.11.more_ref.two_ref, f32[2,8,512]{2,1,0:T(8,128)S(1)} %get-tuple-element.16.one_ref.refs_0_, ...), custom_call_target="tpu_custom_call" | custom-call | flops 4294967296 | bytes 20971520 | tf_op jit(solution)/shard_map/pallas_call | solution.py:272
  132.4 0.1 collective-permute-start.12
  132.5 10.2 %shard_map.55.after_ref = f32[1,1032,256]{2,1,0:T(8,128)S(1)} custom-call(s32[3]{0:T(128)S(1)} %get-tuple-element.23.pos_ref, f32[2,8,512]{2,1,0:T(8,128)S(1)} %shard_map.53.stat_ref.refs_5_.one_ref, f32[2,8,512]{2,1,0:T(8,128)S(1)} %collective-permute-done.11.more_ref.two_ref, f32[2,8,512]{2,1,0:T(8,128)S(1)} %get-tuple-element.16.one_ref.refs_0_, ...), custom_call_target="tpu_custom_call" | custom-call | flops 2147483648 | bytes 18874368 | tf_op jit(solution)/shard_map/pallas_call | solution.py:272
  142.7 0.6 collective-permute-start.13
  143.2 0.0 collective-permute-done.12.theirs_ref
  143.2 0.8 shard_map.56.refs_5_
  144.0 1.7 %collective-permute-start.14 = (bf16[1040,256]{1,0:T(8,128)(2,1)S(1)}, bf16[1040,256]{1,0:T(8,128)(2,1)S(1)}, u32[]{:S(2)}, u32[]{:S(2)}) collective-permute-start(bf16[1040,256]{1,0:T(8,128)(2,1)S(1)} %bitcast.17), channel_id=1, source_target_pairs={{0,16},{8,24},{16,0},{24,8},{1,17},{9,25},{17,1},{25,9},{2,18},{10... | collective-permute-start | bytes 1597448 | tf_op jit(solution)/shard_map/ppermute | solution.py:424
  145.7 0.6 copy.4
  146.3 10.0 %shard_map.57 = f32[1,1032,256]{2,1,0:T(8,128)S(1)} custom-call(s32[3]{0:T(128)S(1)} %get-tuple-element.22.pos_ref, f32[2,8,512]{2,1,0:T(8,128)S(1)} %shard_map.53.stat_ref.refs_5_.one_ref, f32[2,8,512]{2,1,0:T(8,128)S(1)} %collective-permute-done.11.more_ref.two_ref, f32[2,8,512]{2,1,0:T(8,128)S(1)} %get-tuple-element.16.one_ref.refs_0_, ...), custom_call_target="tpu_custom_call" | custom-call | flops 2147483648 | bytes 18874368 | tf_op jit(solution)/shard_map/pallas_call | solution.py:272
  156.3 0.0 collective-permute-done.13
  156.3 1.8 %collective-permute-done.14.refs_0_ = bf16[1040,256]{1,0:T(8,128)(2,1)S(1)} collective-permute-done((bf16[1040,256]{1,0:T(8,128)(2,1)S(1)}, bf16[1040,256]{1,0:T(8,128)(2,1)S(1)}, u32[]{:S(2)}, u32[]{:S(2)}) %collective-permute-start.14) | collective-permute-done | bytes 532512 | tf_op jit(solution)/shard_map/ppermute | solution.py:424
  158.1 2.0 %shard_map.58 = f32[1024,256]{1,0:T(8,128)} custom-call(f32[1032,256]{1,0:T(8,128)S(1)} %bitcast.15, f32[1032,256]{1,0:T(8,128)S(1)} %bitcast.19, bf16[1040,256]{1,0:T(8,128)(2,1)S(1)} %collective-permute-done.14.refs_0_), custom_call_target="tpu_custom_call" | custom-call | flops 7864320 | bytes 3670016 | tf_op jit(solution)/shard_map/pallas_call | solution.py:378
  (6 shorter events, 0.1 us)
Async XLA Ops:
  19.6 4.9 %collective-permute-start = (f32[2,8,512]{2,1,0:T(8,128)S(1)}, f32[2,8,512]{2,1,0:T(8,128)S(1)}, u32[]{:S(2)}, u32[]{:S(2)}) collective-permute-start(f32[2,8,512]{2,1,0:T(8,128)S(1)} %get-tuple-element.12.one_ref.refs_0_), channel_id=1, source_target_pairs={{0,1},{1,0},{2,3},{3,2},{4,5},{5,4},{6,7},{7,6},{8,9},{9,8},{10,11... | collective-permute-start | bytes 98312 | tf_op jit(solution)/shard_map/ppermute | solution.py:436
  24.5 4.1 %collective-permute-start.1 = (f32[2,8,512]{2,1,0:T(8,128)S(1)}, f32[2,8,512]{2,1,0:T(8,128)S(1)}, u32[]{:S(2)}, u32[]{:S(2)}) collective-permute-start(f32[2,8,512]{2,1,0:T(8,128)S(1)} %shard_map.42.one_ref), channel_id=1, source_target_pairs={{0,2},{1,3},{2,0},{3,1},{4,6},{5,7},{6,4},{7,5},{8,10},{9,11},{10,... | collective-permute-start | bytes 98312 | tf_op jit(solution)/shard_map/ppermute | solution.py:436
  28.6 5.0 %collective-permute-start.2 = (f32[2,8,512]{2,1,0:T(8,128)S(1)}, f32[2,8,512]{2,1,0:T(8,128)S(1)}, u32[]{:S(2)}, u32[]{:S(2)}) collective-permute-start(f32[2,8,512]{2,1,0:T(8,128)S(1)} %shard_map.43.stat_ref.refs_3_), channel_id=1, source_target_pairs={{0,4},{1,5},{2,6},{3,7},{4,0},{5,1},{6,2},{7,3},{8,12},{9,13},{10,... | collective-permute-start | bytes 98312 | tf_op jit(solution)/shard_map/ppermute | solution.py:436
  44.0 8.9 %collective-permute-start.3 = (f32[1,264,1024]{2,1,0:T(8,128)S(1)}, f32[1,264,1024]{2,1,0:T(8,128)S(1)}, u32[]{:S(2)}, u32[]{:S(2)}) collective-permute-start(f32[1,264,1024]{2,1,0:T(8,128)S(1)} %get-tuple-element.15.refs_3_), channel_id=1, source_target_pairs={{0,8},{8,0},{16,24},{24,16},{1,9},{9,1},{17,25},{25,17},{2,10},{10... | collective-permute-start | bytes 3244040 | tf_op jit(solution)/shard_map/ppermute | solution.py:420
  52.4 11.3 %collective-permute-start.4 = (f32[1,264,1024]{2,1,0:T(8,128)S(1)}, f32[1,264,1024]{2,1,0:T(8,128)S(1)}, u32[]{:S(2)}, u32[]{:S(2)}) collective-permute-start(f32[1,264,1024]{2,1,0:T(8,128)S(1)} %shard_map.45.after_ref), channel_id=1, source_target_pairs={{0,8},{8,0},{16,24},{24,16},{1,9},{9,1},{17,25},{25,17},{2,10},{10... | collective-permute-start | bytes 3244040 | tf_op jit(solution)/shard_map/ppermute | solution.py:420
  53.6 14.7 %collective-permute-start.5 = (bf16[272,1024]{1,0:T(8,128)(2,1)S(1)}, bf16[272,1024]{1,0:T(8,128)(2,1)S(1)}, u32[]{:S(2)}, u32[]{:S(2)}) collective-permute-start(bf16[272,1024]{1,0:T(8,128)(2,1)S(1)} %bitcast.16), channel_id=1, source_target_pairs={{0,16},{8,24},{16,0},{24,8},{1,17},{9,25},{17,1},{25,9},{2,18},{10... | collective-permute-start | bytes 1671176 | tf_op jit(solution)/shard_map/ppermute | solution.py:424
  69.3 13.2 %collective-permute-start.7 = (bf16[256,1024]{1,0:T(8,128)(2,1)S(1)}, bf16[256,1024]{1,0:T(8,128)(2,1)S(1)}, u32[]{:S(2)}, u32[]{:S(2)}) collective-permute-start(bf16[256,1024]{1,0:T(8,128)(2,1)S(1)} %shard_map.48.refs_0_), channel_id=1, source_target_pairs={{0,16},{8,24},{16,0},{24,8},{1,17},{9,25},{17,1},{25,9},{2,18},{10... | collective-permute-start | bytes 1572872 | tf_op jit(solution)/shard_map/ppermute | solution.py:424
  71.1 11.5 %collective-permute-start.6 = (bf16[256,1024]{1,0:T(8,128)(2,1)S(1)}, bf16[256,1024]{1,0:T(8,128)(2,1)S(1)}, u32[]{:S(2)}, u32[]{:S(2)}) collective-permute-start(bf16[256,1024]{1,0:T(8,128)(2,1)S(1)} %shard_map.48.refs_0_), channel_id=1, source_target_pairs={{0,8},{8,0},{16,24},{24,16},{1,9},{9,1},{17,25},{25,17},{2,10},{10... | collective-permute-start | bytes 1572872 | tf_op jit(solution)/shard_map/ppermute | solution.py:420
  82.5 12.7 %collective-permute-start.8 = (bf16[256,1024]{1,0:T(8,128)(2,1)S(1)}, bf16[256,1024]{1,0:T(8,128)(2,1)S(1)}, u32[]{:S(2)}, u32[]{:S(2)}) collective-permute-start(bf16[256,1024]{1,0:T(8,128)(2,1)S(1)} %collective-permute-done.7.refs_0_), channel_id=1, source_target_pairs={{0,8},{8,0},{16,24},{24,16},{1,9},{9,1},{17,25},{25,17},{2,10},{10... | collective-permute-start | bytes 1572872 | tf_op jit(solution)/shard_map/ppermute | solution.py:420
  107.8 4.0 %collective-permute-start.9 = (f32[2,8,512]{2,1,0:T(8,128)S(1)}, f32[2,8,512]{2,1,0:T(8,128)S(1)}, u32[]{:S(2)}, u32[]{:S(2)}) collective-permute-start(f32[2,8,512]{2,1,0:T(8,128)S(1)} %shard_map.51.one_ref), channel_id=1, source_target_pairs={{0,1},{1,0},{2,3},{3,2},{4,5},{5,4},{6,7},{7,6},{8,9},{9,8},{10,11... | collective-permute-start | bytes 98312 | tf_op jit(solution)/shard_map/ppermute | solution.py:436
  111.8 4.0 %collective-permute-start.10 = (f32[2,8,512]{2,1,0:T(8,128)S(1)}, f32[2,8,512]{2,1,0:T(8,128)S(1)}, u32[]{:S(2)}, u32[]{:S(2)}) collective-permute-start(f32[2,8,512]{2,1,0:T(8,128)S(1)} %shard_map.52.one_ref), channel_id=1, source_target_pairs={{0,2},{1,3},{2,0},{3,1},{4,6},{5,7},{6,4},{7,5},{8,10},{9,11},{10,... | collective-permute-start | bytes 98312 | tf_op jit(solution)/shard_map/ppermute | solution.py:436
  115.8 4.9 %collective-permute-start.11 = (f32[2,8,512]{2,1,0:T(8,128)S(1)}, f32[2,8,512]{2,1,0:T(8,128)S(1)}, u32[]{:S(2)}, u32[]{:S(2)}) collective-permute-start(f32[2,8,512]{2,1,0:T(8,128)S(1)} %shard_map.53.stat_ref.refs_5_.one_ref), channel_id=1, source_target_pairs={{0,4},{1,5},{2,6},{3,7},{4,0},{5,1},{6,2},{7,3},{8,12},{9,13},{10,... | collective-permute-start | bytes 98312 | tf_op jit(solution)/shard_map/ppermute | solution.py:436
  132.4 10.8 %collective-permute-start.12 = (f32[1,1032,256]{2,1,0:T(8,128)S(1)}, f32[1,1032,256]{2,1,0:T(8,128)S(1)}, u32[]{:S(2)}, u32[]{:S(2)}) collective-permute-start(f32[1,1032,256]{2,1,0:T(8,128)S(1)} %get-tuple-element.21.refs_5_), channel_id=1, source_target_pairs={{0,8},{8,0},{16,24},{24,16},{1,9},{9,1},{17,25},{25,17},{2,10},{10... | collective-permute-start | bytes 3170312 | tf_op jit(solution)/shard_map/ppermute | solution.py:420
  142.7 13.6 %collective-permute-start.13 = (f32[1,1032,256]{2,1,0:T(8,128)S(1)}, f32[1,1032,256]{2,1,0:T(8,128)S(1)}, u32[]{:S(2)}, u32[]{:S(2)}) collective-permute-start(f32[1,1032,256]{2,1,0:T(8,128)S(1)} %shard_map.55.after_ref), channel_id=1, source_target_pairs={{0,8},{8,0},{16,24},{24,16},{1,9},{9,1},{17,25},{25,17},{2,10},{10... | collective-permute-start | bytes 3170312 | tf_op jit(solution)/shard_map/ppermute | solution.py:420
  144.0 14.1 %collective-permute-start.14 = (bf16[1040,256]{1,0:T(8,128)(2,1)S(1)}, bf16[1040,256]{1,0:T(8,128)(2,1)S(1)}, u32[]{:S(2)}, u32[]{:S(2)}) collective-permute-start(bf16[1040,256]{1,0:T(8,128)(2,1)S(1)} %bitcast.17), channel_id=1, source_target_pairs={{0,16},{8,24},{16,0},{24,8},{1,17},{9,25},{17,1},{25,9},{2,18},{10... | collective-permute-start | bytes 1597448 | tf_op jit(solution)/shard_map/ppermute | solution.py:424

commit v3 on v0

v3 whole, which is shorter than its diff:
```python
import functools

import jax
import jax.numpy as jnp
from jax import lax
from jax.experimental import pallas as pl
from jax.experimental.pallas import tpu as pltpu
from jax.sharding import PartitionSpec as P

ITERS = 2
F32 = jnp.float32
BF16 = jnp.bfloat16
LOAD_VMEM = 38
SCORE_VMEM = 34
WEIGH_VMEM = 34
LEVELS = 30000.0
LOWEST = -117.0


def divisor(total, wanted):
    size = min(total, wanted)
    while total % size:
        size -= 1
    return size


def round_up(value, unit):
    return -(-value // unit) * unit


def normalize_rows(rows):
    return rows * lax.rsqrt(jnp.sum(rows * rows, axis=1, keepdims=True) + 1e-06)


CORES = 2


def place():
    me = lax.axis_index("pts")
    return lax.div(me, CORES), lax.rem(me, CORES)


def params(mebibytes):
    return pltpu.CompilerParams(vmem_limit_bytes=mebibytes * 2**20)


VMEM = pl.BlockSpec(memory_space=pltpu.VMEM)
ANY = pl.BlockSpec(memory_space=pl.ANY)


def merge(stats, other):
    top = jnp.maximum(stats[0], other[0])
    return top, stats[1] * jnp.exp(stats[0] - top) + other[1] * jnp.exp(other[0] - top)


def to_column(row, height):
    return jnp.broadcast_to(row, (128, height)).T


def encode(values, scale):
    steps = jnp.floor(jnp.abs(values) * (LEVELS / scale) + 0.5)
    power = jnp.floor(steps * (1.0 / 128.0))
    size = (1.0 + (steps * (1.0 / 128.0) - power)) * jnp.exp2(power + LOWEST)
    return jnp.where(values < 0.0, -size, size).astype(BF16)


def decode(codes, scale):
    wide = codes.astype(F32)
    size = jnp.abs(wide)
    power = jnp.floor(jnp.log2(size))
    steps = 128.0 * (power - LOWEST + (size * jnp.exp2(-power) - 1.0))
    return jnp.where(wide < 0.0, -steps, steps) * (scale * (1.0 / LEVELS))


def load_body(c_hbm, sums_ref, x_hbm, x_ref, units_ref, rows_ref, row_sems, point_sem):
    row_step = rows_ref.shape[0] // row_sems.shape[0]

    def rows_of(number):
        part = pl.ds(number * row_step, row_step)
        return pltpu.make_async_copy(c_hbm.at[part, :], rows_ref.at[part, :], row_sems.at[number])

    all_points = pltpu.make_async_copy(x_hbm, x_ref, point_sem)
    for number in range(row_sems.shape[0]):
        rows_of(number).start()
    all_points.start()
    for number in range(row_sems.shape[0]):
        rows_of(number).wait()
        part = slice(number * row_step, (number + 1) * row_step)
        scale = to_column(lax.rsqrt(sums_ref[:, part] + 1e-06), row_step)[:, 0:1]
        units_ref[part, :] = (rows_ref[part, :] * scale).astype(BF16)
    all_points.wait()


def load(centroids, points):
    square_sums = jnp.sum(centroids * centroids, axis=1)[None]
    return pl.pallas_call(
        load_body,
        in_specs=[ANY, VMEM, ANY],
        out_specs=[VMEM] * 2,
        out_shape=[
            jax.ShapeDtypeStruct(points.shape, BF16),
            jax.ShapeDtypeStruct(centroids.shape, BF16),
        ],
        scratch_shapes=[
            pltpu.VMEM(centroids.shape, F32),
            pltpu.SemaphoreType.DMA((divisor(centroids.shape[0] // 16, 4),)),
            pltpu.SemaphoreType.DMA(()),
        ],
        compiler_params=params(LOAD_VMEM),
        cost_estimate=pl.CostEstimate(
            flops=4 * centroids.size, bytes_accessed=4 * centroids.size + 2 * points.size, transcendentals=0
        ),
    )(centroids, square_sums, points)


def score_points(raw, units, x_ref, e_parts, stat_ref, stage, semaphores):
    line = stat_ref.shape[2]
    lines = stage.shape[0]
    sub = divisor(line, 256)

    def copies(number, slot):
        columns = pl.ds(pl.multiple_of(number * line, line), line)
        return [
            pltpu.make_async_copy(stage.at[slot, rows, :], target(columns), semaphores.at[slot, part])
            for part, (rows, target) in enumerate(e_parts)
        ]

    def visit(step, carry):
        for slot in range(lines):
            number = step * lines + slot

            @pl.when(step > 0)
            def _():
                for copy in copies(number - lines, slot):
                    copy.wait()

            tops, totals = [], []
            for offset in range(0, line, sub):
                logits = lax.dot_general(
                    units[...],
                    x_ref[pl.ds(pl.multiple_of(number * line + offset, sub), sub), :],
                    (((1,), (1,)), ((), ())),
                    preferred_element_type=F32,
                )
                top = jnp.max(logits, axis=0, keepdims=True)
                shifted = jnp.exp(logits - top)
                stage[slot, :, offset : offset + sub] = logits if raw else shifted
                tops.append(top)
                totals.append(jnp.sum(shifted, axis=0, keepdims=True))
            stat_ref[0, pl.ds(number, 1), :] = jnp.concatenate(tops, axis=1)
            stat_ref[1, pl.ds(number, 1), :] = jnp.concatenate(totals, axis=1)
            for copy in copies(number, slot):
                copy.start()
        return carry

    steps = stat_ref.shape[1] // lines
    lax.fori_loop(0, steps, visit, 0)
    for slot in range(lines):
        for copy in copies((steps - 1) * lines + slot, slot):
            copy.wait()


def stat_shape(total):
    line = divisor(total, 512)
    return (2, total // line, line)


def first_scores_body(raw, units, x_ref, _, e_hbm, stat_ref, stage, semaphores):
    target = [(slice(None), lambda columns: e_hbm.at[:, columns])]
    score_points(raw, units, x_ref, target, stat_ref, stage, semaphores)


def next_scores_body(raw, count, away, *refs):
    unit_refs = refs[:count]
    x_ref = refs[count]
    e_hbm, stat_ref, units, stage, semaphores = refs[-5:]
    rows = unit_refs[0].shape[0]
    pair = CORES * rows
    chip, core = place()
    chips = e_hbm.shape[0] // pair
    for number, ref in enumerate(unit_refs):
        of_pair = core if number % CORES == 0 else 1 - core
        start = pl.multiple_of((number - number % CORES + of_pair) * rows, rows)
        units[pl.ds(start, rows), :] = ref[...]

    def target_of(number):
        start = pl.multiple_of(lax.rem(chip + away + number, chips) * pair, pair)
        return lambda columns: e_hbm.at[pl.ds(start, pair), columns]

    targets = [
        (slice(number * pair, (number + 1) * pair), target_of(number)) for number in range(count // CORES)
    ]
    score_points(raw, units, x_ref, targets, stat_ref, stage, semaphores)


def scores(raw, blocks, points, away=None, shifted=None):
    total, width = points.shape
    count = len(blocks)
    rows = sum(block.shape[0] for block in blocks)
    all_rows = rows if shifted is None else shifted.shape[0]
    stat = stat_shape(total)
    parts = 1 if away is None else count // CORES
    more = [] if shifted is None or away == 0 else [shifted]
    scratch = [
        pltpu.VMEM((divisor(stat[1], 2), rows, stat[2]), F32),
        pltpu.SemaphoreType.DMA((divisor(stat[1], 2), parts)),
    ]
    if away is not None:
        scratch = [pltpu.VMEM((rows, width), BF16)] + scratch
    if away is None:
        body = functools.partial(first_scores_body, raw)
    else:
        body = functools.partial(next_scores_body, raw, count, away)
    return pl.pallas_call(
        body,
        in_specs=[VMEM] * (count + 1) + [ANY] * len(more),
        out_specs=[VMEM, ANY, VMEM],
        out_shape=[
            jax.ShapeDtypeStruct(points.shape, BF16),
            jax.ShapeDtypeStruct((all_rows, total), F32),
            jax.ShapeDtypeStruct(stat, F32),
        ],
        input_output_aliases={count + number: number for number in range(1 + len(more))},
        scratch_shapes=scratch,
        compiler_params=params(SCORE_VMEM),
        cost_estimate=pl.CostEstimate(
            flops=2 * rows * total * width,
            bytes_accessed=2 * total * width + 4 * rows * total,
            transcendentals=rows * total,
        ),
    )(*blocks, points, *more)


FAR, THEIRS, OWN = range(3)


def weigh_body(by_rows, n_tops, kind, others, extra, pair, stat_ref, more_ref, *refs):
    parts = CORES if kind == FAR else 1
    top_refs, (e_hbm, x_ref, _), refs = refs[:n_tops], refs[n_tops : n_tops + 3], refs[n_tops + 3 :]
    out_refs, refs = refs[:parts], refs[parts + 1 :]
    scale_refs, refs = refs[:2], refs[2:]
    weights_refs, (stage, mass_ref, sum_ref, semaphores) = refs[:2], refs[2:]
    chip, core = place()
    line = stat_ref.shape[2]
    total = x_ref.shape[0]
    height, span = sum_ref.shape
    slots, _, chunk = stage.shape
    steps = total // chunk
    lanes = min(line, 128)

    def block_of(other):
        if kind == FAR:
            return lax.rem(chip + 1 + other, others + 1)
        return chip * CORES + (core if kind == OWN else 1 - core)

    def copy_of(number):
        other, step = divmod(number, steps)
        rows = pl.ds(pl.multiple_of(block_of(other) * height, height), height) if by_rows else slice(None)
        columns = slice(step * chunk, (step + 1) * chunk)
        slot = number % slots
        return pltpu.make_async_copy(e_hbm.at[rows, columns], stage.at[slot], semaphores.at[slot])

    for number in range(min(slots, others * steps)):
        copy_of(number).start()
    top, all_total = merge(stat_ref, more_ref)
    if by_rows:
        scale_refs[0][...] = top
        scale_refs[1][...] = 1.0 / all_total
    else:
        for ref, scale_ref in zip((top_refs[0], top_refs[-1]), scale_refs):
            scale_ref[...] = jnp.exp(ref[0] - top) / all_total

    def weights_of(values, group, number):
        one, two = (ref[number : number + 1, :] for ref in scale_refs)
        if by_rows:
            return jnp.exp(values - one) * two
        return values * jnp.where(chip == group, one, two)

    group_rows = height if by_rows else pair
    for number in range(others * steps):
        other, step = divmod(number, steps)
        slot = number % slots
        weights_ref = weights_refs[step % 2]
        copy_of(number).wait()
        for group in range(height // group_rows):
            rows = slice(group * group_rows, (group + 1) * group_rows)
            mass = None
            for offset in range(0, chunk, line):
                values = stage[slot, rows, offset : offset + line]
                weights = weights_of(values, group, (step * chunk + offset) // line).astype(BF16)
                weights_ref[rows, offset : offset + line] = weights
                wide = weights.astype(F32)
                for lane in range(0, line, lanes):
                    piece = wide[:, lane : lane + lanes]
                    mass = piece if mass is None else mass + piece
            mass_ref[rows, :] = mass if step == 0 else mass_ref[rows, :] + mass
        if number + slots < others * steps:
            copy_of(number + slots).start()
        columns = slice(None)
        if not by_rows:
            columns = pl.ds(pl.multiple_of(block_of(other) * span, span), span)
        product = jnp.dot(
            weights_ref[...],
            x_ref[step * chunk : (step + 1) * chunk, columns],
            preferred_element_type=F32,
        )
        sum_ref[...] = product if step == 0 else sum_ref[...] + product
        if step < steps - 1:
            continue

        rows = out_refs[0].shape[1] - extra
        width = out_refs[0].shape[2]
        mass = jnp.sum(mass_ref[...].T, axis=0, keepdims=True)
        for part, ref in enumerate(out_refs):
            side = lax.rem(core + part, parts)
            ref[other, rows:, :] = jnp.zeros((extra, width), F32)
            if by_rows:
                found = mass
                if parts > 1:
                    found = jnp.where(side == 0, mass[:, :rows], mass[:, rows:])
                    ref[other, :rows, :] = sum_ref[pl.ds(pl.multiple_of(side * rows, rows), rows), :]
                else:
                    ref[other, :rows, :] = sum_ref[...]
                ref[other, rows : rows + 1, :rows] = found
            else:
                sums = sum_ref[...]
                if parts > 1:
                    sums = jnp.where(side == 0, sums[:, :width], sums[:, width:])
                ref[other, :rows, :] = sums
                for line_number in range(rows // width):
                    ref[other, rows + line_number : rows + line_number + 1, :] = mass[
                        :, line_number * width : (line_number + 1) * width
                    ]


def weigh(by_rows, kind, chips, stats, tops, shifted, points, after):
    total, width = points.shape
    pair = shifted.shape[0] // chips
    parts, others = (CORES, chips - 1) if kind == FAR else (1, 1)
    line = stats[0].shape[2]
    chunk = line * divisor(total // line, 2)
    if by_rows:
        rows, cols = pair // CORES, width
        sums = (rows * parts, width)
    else:
        rows, cols = shifted.shape[0], width // (CORES * chips)
        sums = (rows, cols * parts)
    n_tops = len(tops)
    extra = round_up(-(-rows // cols), 8)
    return pl.pallas_call(
        functools.partial(weigh_body, by_rows, n_tops, kind, others, extra, pair),
        in_specs=[VMEM] * (2 + n_tops) + [ANY, VMEM, ANY],
        out_specs=[VMEM] * (parts + 1),
        input_output_aliases={3 + n_tops: parts},
        scratch_shapes=[pltpu.VMEM(stats[0].shape[1:], F32)] * 2
        + [pltpu.VMEM((sums[0], chunk), BF16)] * 2
        + [
            pltpu.VMEM((2, sums[0], chunk), F32),
            pltpu.VMEM((sums[0], 128), F32),
            pltpu.VMEM(sums, F32),
            pltpu.SemaphoreType.DMA((2,)),
        ],
        out_shape=[jax.ShapeDtypeStruct((others, rows + extra, cols), F32)] * parts
        + [jax.ShapeDtypeStruct(points.shape, BF16)],
        compiler_params=params(WEIGH_VMEM),
        cost_estimate=pl.CostEstimate(
            flops=2 * others * sums[0] * sums[1] * total,
            bytes_accessed=2 * others * total * (sums[1] + 2 * sums[0]),
            transcendentals=0,
        ),
    )(*stats, *tops, shifted, points, after)


def fold_body(rows, lines, mine_ref, theirs_ref, after_ref, out_ref):
    width = out_ref.shape[1]
    step = divisor(rows, 128) if lines == 1 else width
    out_ref[rows:, :] = jnp.zeros((out_ref.shape[0] - rows, width), BF16)
    scales = []
    for start in range(0, rows, step):
        part = slice(start, start + step)
        total = mine_ref[part, :] + theirs_ref[part, :]
        top = jnp.max(jnp.abs(total), axis=1, keepdims=True)
        scale = jnp.maximum(top * 1.01, 1e-30).astype(BF16)
        out_ref[part, :] = encode(total, scale.astype(F32))
        scales.append(jnp.broadcast_to(scale.astype(F32), (step, 128)).T[0:1, :])
    mass = mine_ref[rows : rows + lines, :] + theirs_ref[rows : rows + lines, :]
    if lines == 1:
        out_ref[rows : rows + 1, :rows] = jnp.concatenate(scales, axis=1).astype(BF16)
    else:
        out_ref[rows : rows + lines, :] = jnp.concatenate(scales, axis=0).astype(BF16)
    for number in range(1, 4):
        rounded = mass.astype(BF16)
        out_ref[rows + number * lines : rows + (number + 1) * lines, :] = rounded
        mass = mass - rounded.astype(F32)


def fold(mine, theirs, after):
    others, height, width = mine.shape
    out_height = coded_height(height, width)
    return pl.pallas_call(
        functools.partial(fold_body, *shape_of(height, width)),
        grid=(others,),
        in_specs=[pl.BlockSpec((None, height, width), lambda d: (d, 0, 0))] * 2 + [ANY],
        out_specs=pl.BlockSpec((None, out_height, width), lambda d: (d, 0, 0)),
        out_shape=jax.ShapeDtypeStruct((others, out_height, width), BF16),
        compiler_params=params(10),
        cost_estimate=pl.CostEstimate(
            flops=20 * others * height * width,
            bytes_accessed=10 * others * height * width,
            transcendentals=others * height * width,
        ),
    )(mine, theirs, after)


def shape_of(height, width):
    rows = height - 8
    while rows + round_up(-(-rows // width), 8) != height:
        rows -= 8
    return rows, -(-rows // width)


def coded_height(height, width):
    rows, lines = shape_of(height, width)
    return rows + round_up(4 * lines, 16)


def finish_body(rows, lines, as_units, mine_ref, theirs_ref, *refs):
    code_refs, out_ref = refs[:-1], refs[-1]
    width = out_ref.shape[1]
    step = divisor(rows, 128) if lines == 1 else width
    mass = mine_ref[rows : rows + lines, :] + theirs_ref[rows : rows + lines, :]
    for ref in code_refs:
        for number in range(1, 4):
            start = rows + number * lines
            mass = mass + ref[start : start + lines, :].astype(F32)

    def column(values, number):
        if lines == 1:
            line = values[:, number * step : (number + 1) * step]
        else:
            line = values[number : number + 1, :]
        return to_column(line, step)[:, 0:1]

    scales = [ref[rows : rows + lines, :].astype(F32) for ref in code_refs]
    for number in range(rows // step):
        part = slice(number * step, (number + 1) * step)
        total = mine_ref[part, :] + theirs_ref[part, :]
        for ref, scale in zip(code_refs, scales):
            total = total + decode(ref[part, :], column(scale, number))
        means = total / jnp.maximum(column(mass, number), 1.0)
        out_ref[part, :] = normalize_rows(means).astype(BF16) if as_units else means


def finish(as_units, mine, theirs, codes):
    height, width = mine.shape
    rows, lines = shape_of(height, width)
    out_type = BF16 if as_units else F32
    return pl.pallas_call(
        functools.partial(finish_body, rows, lines, as_units),
        out_shape=jax.ShapeDtypeStruct((rows, width), out_type),
        compiler_params=params(10),
        cost_estimate=pl.CostEstimate(
            flops=30 * rows * width,
            bytes_accessed=(12 + 2 * len(codes)) * rows * width,
            transcendentals=2 * rows * width,
        ),
    )(mine, theirs, *codes)


def keep_body(value_ref, after_ref, out_ref):
    pass


def keep_until(value, after):
    return pl.pallas_call(
        keep_body,
        in_specs=[VMEM, ANY],
        out_specs=VMEM,
        out_shape=jax.ShapeDtypeStruct(value.shape, value.dtype),
        input_output_aliases={0: 0},
        compiler_params=params(10),
    )(value, after)


def merge_body(one_ref, two_ref, out_ref):
    out_ref[0], out_ref[1] = merge(one_ref, two_ref)


def merged(one, two):
    return pl.pallas_call(
        merge_body, out_shape=jax.ShapeDtypeStruct(one.shape, F32), compiler_params=params(10)
    )(one, two)


def log_body(one_ref, two_ref, out_ref):
    top, total = merge(one_ref, two_ref)
    out_ref[...] = top + jnp.log(total)


def log_norms(one, two):
    return pl.pallas_call(
        log_body, out_shape=jax.ShapeDtypeStruct(one.shape[1:], F32), compiler_params=params(10)
    )(one, two).reshape(-1)


def on_device(n_pts, n_cen, points, centroids):
    chips = n_pts // CORES

    def to_partner(value):
        return lax.ppermute(value, "pts", [(i, i ^ 1) for i in range(n_pts)])

    def to_chip(value, away):
        moves = [(i, (i + CORES * away) % n_pts) for i in range(n_pts)]
        return lax.ppermute(value, "pts", moves)

    def over_centroids(stats):
        if n_cen & (n_cen - 1):
            found = [stats]
            for away in range(1, n_cen):
                moves = [(i, (i + away) % n_cen) for i in range(n_cen)]
                found.append(lax.ppermute(stats, "cen", moves))
            return functools.reduce(merged, found[:-1]), found[-1]
        away = 1
        while True:
            moves = [(i, i ^ away) for i in range(n_cen)]
            other = lax.ppermute(stats, "cen", moves)
            away *= 2
            if away >= n_cen:
                return stats, other
            stats = merged(stats, other)

    def sums_over_pts(by_rows, stats, tops, shifted, points):
        def weighted(kind, after):
            nonlocal points
            *found, points = weigh(by_rows, kind, chips, stats, tops, shifted, points, after)
            return found

        far_mine, far_theirs = weighted(FAR, stats[0])
        far_found = to_partner(far_theirs)
        (near_theirs,) = weighted(THEIRS, far_theirs)
        near_found = to_partner(near_theirs)
        coded = fold(far_mine, far_found, near_theirs)
        codes = [to_chip(coded[away - 1], away) for away in range(1, chips)]
        (near_mine,) = weighted(OWN, coded)
        return finish(by_rows, near_mine[0], near_found[0], codes), points

    points, units = load(centroids, points)
    points, shifted, own = scores(ITERS > 1, [units], points)
    stats = over_centroids(own)
    tops = [own]
    for iteration in range(1, ITERS):
        raw = iteration + 1 < ITERS
        mine, points = sums_over_pts(True, stats, tops, shifted, points)
        away_units = [to_chip(mine, -away) for away in range(1, chips)]
        points, shifted, near_own = scores(raw, [mine, to_partner(mine)], points, 0, shifted)
        away_units = [keep_until(unit, near_own) for unit in away_units]
        blocks = [unit for mine in away_units for unit in (mine, to_partner(mine))]
        points, shifted, far_own = scores(raw, blocks, points, 1, shifted)
        tops = [near_own, far_own]
        stats = over_centroids(merged(near_own, far_own))
    means, _ = sums_over_pts(False, stats, tops, shifted, points)
    return (means, log_norms(*stats))


def solution(mesh):
    placed = (P("pts", None), P("cen", None))
    return jax.shard_map(
        functools.partial(on_device, mesh.shape["pts"], mesh.shape["cen"]),
        mesh=mesh,
        in_specs=placed,
        out_specs=(P("cen", "pts"), P("pts")),
        check_vma=False,
    )
```

time: 372 us -> 137 us (0.37)
  blocking collectives: 159 us -> 0 us
  Pallas kernels: 0 us -> 81.2 us
  matrix products: 69.5 us -> 0 us
  waiting for transfers between devices: 82.1 us -> 29.1 us
  other arithmetic: 40.3 us -> 2.68 us
  starting transfers between devices: 0.3 us -> 21.7 us
  between operations: 13.8 us -> 0.81 us
  local copies, waits for them, and re-layouts: 6.43 us -> 1.37 us
    psum x5 -> x0, blocking collectives: 83.3 us -> none  [the longest x2 66.2 us: on_device(): row_total = lax.psum(jnp.sum(shifted, axis=1), 'cen')]
    pallas_call x0 -> x21, Pallas kernels: none -> 81.2 us  [the longest x6 40.5 us: weigh(): pl.pallas_call(functools.partial(weigh_body, by_rows, n_tops, kind, other...]
    pmax x2 -> x0, blocking collectives: 75.9 us -> none  [on_device(): row_max = lax.pmax(local_max, 'cen')]
    dot_general x6 -> x0, matrix products: 69.5 us -> none  [the longest x2 31.9 us: on_device(): lax.dot_general(points, unit_rows, (((1,), (1,)), ((), ())), preferred_el...]
    reduce_scatter x2 -> x0, waiting for transfers between devices: 58 us -> none  [on_device(): shares = lax.psum_scatter(weighted, 'pts', scatter_dimension=1, tiled=True)]
    ppermute x0 -> x15, waiting for transfers between devices: none -> 29.1 us  [the longest x3 15.1 us: to_chip(): return lax.ppermute(value, 'pts', moves)]
    all_gather x1 -> x0, waiting for transfers between devices: 24 us -> none  [on_device(): unit_rows = lax.all_gather(unit_shares, 'pts', axis=1, tiled=True)]
    ppermute x0 -> x15, starting transfers between devices: none -> 21.7 us  [the longest x6 14.9 us: over_centroids(): other = lax.ppermute(stats, 'cen', moves)]
  transfers between devices with their start and end apart: 3 -> 15, of which waited for: 3 -> 11; matrix products, arithmetic and copies ran while one was open for 4% -> 0% of each run, Pallas kernels for 0% -> 26%
where the time goes in v3:
time: 137 us
  Pallas kernels  81.2 us (59%)
  waiting for transfers between devices  29.1 us (21%)
  starting transfers between devices  21.7 us (16%)
  other arithmetic  2.68 us (2%)
  local copies, waits for them, and re-layouts  1.37 us (1%)
    pallas_call x6, Pallas kernels, weigh(): pl.pallas_call(functools.partial(weigh_body, by_rows, n_tops, kind, other...  40.5 us
    pallas_call x3, Pallas kernels, scores(): pl.pallas_call(body, in_specs=[VMEM] * (count + 1) + [ANY] * len(more), o...  32.5 us
    ppermute x3, waiting for transfers between devices, to_chip(): return lax.ppermute(value, 'pts', moves)  15.1 us
    ppermute x6, starting transfers between devices, over_centroids(): other = lax.ppermute(stats, 'cen', moves)  14.9 us
    ppermute x6, waiting for transfers between devices, over_centroids(): other = lax.ppermute(stats, 'cen', moves)  12 us
    ppermute x3, starting transfers between devices, to_chip(): return lax.ppermute(value, 'pts', moves)  5.46 us
    pallas_call x1, Pallas kernels, load(): pl.pallas_call(load_body, in_specs=[ANY, VMEM, ANY], out_specs=[VMEM] * 2...  3.7 us
    pallas_call x2, Pallas kernels, finish(): pl.pallas_call(functools.partial(finish_body, rows, lines, as_units), out...  2.96 us
  transfers between devices with their start and end apart: 15, of which 11 were waited for; matrix products, arithmetic and copies ran while one was open for 0% of the time, Pallas kernels for 26%

profile of v3, /device:TPU:0, one launch (start us, length us, event | category | flops | bytes accessed | tf_op | source)
XLA Modules:
  0.0 136.8 jit_solution(13621535837810375890)
XLA Ops:
  0.6 0.0 copy-start
  0.6 2.7 %multiply_reduce_fusion = f32[1024]{0:T(1024)S(1)} fusion(f32[1024,1024]{1,0:T(8,128)} %c_hbm.1), kind=kLoop, calls=%fused_computation | loop fusion | flops 2096128 | bytes 4198400 | tf_op jit(solution)/shard_map/reduce_sum | solution.py:95
  3.3 0.8 copy-done
  4.1 3.7 %shard_map.41 = (bf16[4096,1024]{1,0:T(8,128)(2,1)S(1)}, bf16[1024,1024]{1,0:T(8,128)(2,1)S(1)}) custom-call(f32[1024,1024]{1,0:T(8,128)S(1)} %copy-done, f32[1,1024]{1,0:T(1,128)S(1)} %bitcast.16, bf16[4096,1024]{1,0:T(8,128)(2,1)} %x_hbm.1), custom_call_target="tpu_custom_call" | custom-call | flops 4194304 | bytes 12582912 | tf_op jit(solution)/shard_map/pallas_call | solution.py:96
  7.8 14.3 %shard_map.42 = (bf16[4096,1024]{1,0:T(8,128)(2,1)S(1)}, f32[1024,4096]{1,0:T(8,128)}, f32[2,8,512]{2,1,0:T(8,128)S(1)}) custom-call(bf16[1024,1024]{1,0:T(8,128)(2,1)S(1)} %get-tuple-element.26.units, bf16[4096,1024]{1,0:T(8,128)(2,1)S(1)} %get-tuple-element.27.x_ref), custom_call_target="tpu_custom_call", output_to_operand_aliasing={{0}: (1, {})} | custom-call | flops 8589934592 | bytes 25165824 | tf_op jit(solution)/shard_map/pallas_call | solution.py:214
  22.1 3.0 %collective-permute-start = (f32[2,8,512]{2,1,0:T(8,128)S(1)}, f32[2,8,512]{2,1,0:T(8,128)S(1)}, u32[]{:S(2)}, u32[]{:S(2)}) collective-permute-start(f32[2,8,512]{2,1,0:T(8,128)S(1)} %get-tuple-element.28.one_ref.refs_0_), channel_id=1, source_target_pairs={{0,1},{1,0},{2,3},{3,2},{4,5},{5,4},{6,7},{7,6},{8,9},{9,8},{10,11... | collective-permute-start | bytes 98312 | tf_op jit(solution)/shard_map/ppermute | solution.py:526
  25.2 1.9 %collective-permute-done.two_ref = f32[2,8,512]{2,1,0:T(8,128)S(1)} collective-permute-done((f32[2,8,512]{2,1,0:T(8,128)S(1)}, f32[2,8,512]{2,1,0:T(8,128)S(1)}, u32[]{:S(2)}, u32[]{:S(2)}) %collective-permute-start) | collective-permute-done | bytes 32800 | tf_op jit(solution)/shard_map/ppermute | solution.py:526
  27.1 2.2 %collective-permute-start.1 = (f32[2,8,512]{2,1,0:T(8,128)S(1)}, f32[2,8,512]{2,1,0:T(8,128)S(1)}, u32[]{:S(2)}, u32[]{:S(2)}) collective-permute-start(f32[2,8,512]{2,1,0:T(8,128)S(1)} %shard_map.43.one_ref), channel_id=1, source_target_pairs={{0,2},{1,3},{2,0},{3,1},{4,6},{5,7},{6,4},{7,5},{8,10},{9,11},{10,... | collective-permute-start | bytes 98312 | tf_op jit(solution)/shard_map/ppermute | solution.py:526
  29.2 1.9 %collective-permute-done.1.two_ref = f32[2,8,512]{2,1,0:T(8,128)S(1)} collective-permute-done((f32[2,8,512]{2,1,0:T(8,128)S(1)}, f32[2,8,512]{2,1,0:T(8,128)S(1)}, u32[]{:S(2)}, u32[]{:S(2)}) %collective-permute-start.1) | collective-permute-done | bytes 32800 | tf_op jit(solution)/shard_map/ppermute | solution.py:526
  31.2 3.1 %collective-permute-start.2 = (f32[2,8,512]{2,1,0:T(8,128)S(1)}, f32[2,8,512]{2,1,0:T(8,128)S(1)}, u32[]{:S(2)}, u32[]{:S(2)}) collective-permute-start(f32[2,8,512]{2,1,0:T(8,128)S(1)} %shard_map.44.stat_ref.refs_3_), channel_id=1, source_target_pairs={{0,4},{1,5},{2,6},{3,7},{4,0},{5,1},{6,2},{7,3},{8,12},{9,13},{10,... | collective-permute-start | bytes 98312 | tf_op jit(solution)/shard_map/ppermute | solution.py:526
  34.3 1.9 %collective-permute-done.2.more_ref = f32[2,8,512]{2,1,0:T(8,128)S(1)} collective-permute-done((f32[2,8,512]{2,1,0:T(8,128)S(1)}, f32[2,8,512]{2,1,0:T(8,128)S(1)}, u32[]{:S(2)}, u32[]{:S(2)}) %collective-permute-start.2) | collective-permute-done | bytes 32800 | tf_op jit(solution)/shard_map/ppermute | solution.py:526
  36.2 6.9 %shard_map.45 = (f32[1,264,1024]{2,1,0:T(8,128)S(1)}, f32[1,264,1024]{2,1,0:T(8,128)S(1)}, bf16[4096,1024]{1,0:T(8,128)(2,1)S(1)}) custom-call(f32[2,8,512]{2,1,0:T(8,128)S(1)} %shard_map.44.stat_ref.refs_3_, f32[2,8,512]{2,1,0:T(8,128)S(1)} %collective-permute-done.2.more_ref, ...), custom_call_target="tpu_custom_call", output_to_operand_aliasing={{2}: (4, {})} | custom-call | flops 4294967296 | bytes 16777216 | tf_op jit(solution)/shard_map/pallas_call | solution.py:350
  43.1 0.1 collective-permute-start.3
  43.2 4.4 %shard_map.46 = (f32[1,264,1024]{2,1,0:T(8,128)S(1)}, bf16[4096,1024]{1,0:T(8,128)(2,1)S(1)}) custom-call(f32[2,8,512]{2,1,0:T(8,128)S(1)} %shard_map.44.stat_ref.refs_3_, f32[2,8,512]{2,1,0:T(8,128)S(1)} %collective-permute-done.2.more_ref, f32[2,8,512]{2,1,0:T(8,128)S(1)} %get-tuple-element.28.one_ref.refs_0_, ...), custom_call_target="tpu_custom_call", output_to_operand_aliasing={{1}: (4, {})} | custom-call | flops 2147483648 | bytes 12582912 | tf_op jit(solution)/shard_map/pallas_call | solution.py:350
  47.5 0.6 collective-permute-start.4
  48.1 0.0 collective-permute-done.3.theirs_ref
  48.1 0.7 shard_map.47.refs_3_
  48.8 1.9 %collective-permute-start.5 = (bf16[272,1024]{1,0:T(8,128)(2,1)S(1)}, bf16[272,1024]{1,0:T(8,128)(2,1)S(1)}, u32[]{:S(2)}, u32[]{:S(2)}) collective-permute-start(bf16[272,1024]{1,0:T(8,128)(2,1)S(1)} %bitcast.9), channel_id=1, source_target_pairs={{0,16},{8,24},{16,0},{24,8},{1,17},{9,25},{17,1},{25,9},{2,18},{10... | collective-permute-start | bytes 1671176 | tf_op jit(solution)/shard_map/ppermute | solution.py:514
  50.7 4.4 %shard_map.48 = (f32[1,264,1024]{2,1,0:T(8,128)S(1)}, bf16[4096,1024]{1,0:T(8,128)(2,1)S(1)}) custom-call(f32[2,8,512]{2,1,0:T(8,128)S(1)} %shard_map.44.stat_ref.refs_3_, f32[2,8,512]{2,1,0:T(8,128)S(1)} %collective-permute-done.2.more_ref, f32[2,8,512]{2,1,0:T(8,128)S(1)} %get-tuple-element.28.one_ref.refs_0_, ...), custom_call_target="tpu_custom_call", output_to_operand_aliasing={{1}: (4, {})} | custom-call | flops 2147483648 | bytes 12582912 | tf_op jit(solution)/shard_map/pallas_call | solution.py:350
  55.1 0.0 collective-permute-done.4
  55.1 8.4 %collective-permute-done.5.refs_0_ = bf16[272,1024]{1,0:T(8,128)(2,1)S(1)} collective-permute-done((bf16[272,1024]{1,0:T(8,128)(2,1)S(1)}, bf16[272,1024]{1,0:T(8,128)(2,1)S(1)}, u32[]{:S(2)}, u32[]{:S(2)}) %collective-permute-start.5) | collective-permute-done | bytes 557088 | tf_op jit(solution)/shard_map/ppermute | solution.py:514
  63.5 0.9 shard_map.49.refs_0_
  64.5 0.1 collective-permute-start.6
  64.5 1.8 %collective-permute-start.7 = (bf16[256,1024]{1,0:T(8,128)(2,1)S(1)}, bf16[256,1024]{1,0:T(8,128)(2,1)S(1)}, u32[]{:S(2)}, u32[]{:S(2)}) collective-permute-start(bf16[256,1024]{1,0:T(8,128)(2,1)S(1)} %shard_map.49.refs_0_), channel_id=1, source_target_pairs={{0,16},{8,24},{16,0},{24,8},{1,17},{9,25},{17,1},{25,9},{2,18},{10... | collective-permute-start | bytes 1572872 | tf_op jit(solution)/shard_map/ppermute | solution.py:514
  66.3 0.1 collective-permute-done.6.refs_1_
  66.4 9.2 %shard_map.50 = (bf16[4096,1024]{1,0:T(8,128)(2,1)S(1)}, f32[1024,4096]{1,0:T(8,128)}, f32[2,8,512]{2,1,0:T(8,128)S(1)}) custom-call(bf16[256,1024]{1,0:T(8,128)(2,1)S(1)} %shard_map.49.refs_0_, bf16[256,1024]{1,0:T(8,128)(2,1)S(1)} %collective-permute-done.6.refs_1_, bf16[4096,1024]{1,0:T(8,128)(2,1)S(1)} %get-tuple-element.37.refs_2_), custom_call_target="tpu_custom_call", output_to_operand_aliasing={{0}: (2, {})} | custom-call | flops 4294967296 | bytes 16777216 | tf_op jit(solution)/shard_map/pallas_call | solution.py:214
  75.6 3.3 %collective-permute-done.7.value_ref = bf16[256,1024]{1,0:T(8,128)(2,1)S(1)} collective-permute-done((bf16[256,1024]{1,0:T(8,128)(2,1)S(1)}, bf16[256,1024]{1,0:T(8,128)(2,1)S(1)}, u32[]{:S(2)}, u32[]{:S(2)}) %collective-permute-start.7) | collective-permute-done | bytes 524320 | tf_op jit(solution)/shard_map/ppermute | solution.py:514
  78.9 0.0 collective-permute-start.8
  78.9 1.9 %collective-permute-done.8.refs_1_ = bf16[256,1024]{1,0:T(8,128)(2,1)S(1)} collective-permute-done((bf16[256,1024]{1,0:T(8,128)(2,1)S(1)}, bf16[256,1024]{1,0:T(8,128)(2,1)S(1)}, u32[]{:S(2)}, u32[]{:S(2)}) %collective-permute-start.8) | collective-permute-done | bytes 524320 | tf_op jit(solution)/shard_map/ppermute | solution.py:510
  80.8 8.9 %shard_map.52 = (bf16[4096,1024]{1,0:T(8,128)(2,1)S(1)}, f32[1024,4096]{1,0:T(8,128)}, f32[2,8,512]{2,1,0:T(8,128)S(1)}) custom-call(bf16[256,1024]{1,0:T(8,128)(2,1)S(1)} %shard_map.51.refs_0_, bf16[256,1024]{1,0:T(8,128)(2,1)S(1)} %collective-permute-done.8.refs_1_, ...), custom_call_target="tpu_custom_call", output_to_operand_aliasing={{0}: (2, {}), {1}: (3, {})} | custom-call | flops 4294967296 | bytes 16777216 | tf_op jit(solution)/shard_map/pallas_call | solution.py:214
  89.8 1.8 %collective-permute-start.9 = (f32[2,8,512]{2,1,0:T(8,128)S(1)}, f32[2,8,512]{2,1,0:T(8,128)S(1)}, u32[]{:S(2)}, u32[]{:S(2)}) collective-permute-start(f32[2,8,512]{2,1,0:T(8,128)S(1)} %shard_map.53.one_ref), channel_id=1, source_target_pairs={{0,1},{1,0},{2,3},{3,2},{4,5},{5,4},{6,7},{7,6},{8,9},{9,8},{10,11... | collective-permute-start | bytes 98312 | tf_op jit(solution)/shard_map/ppermute | solution.py:526
  91.6 2.2 %collective-permute-done.9.two_ref = f32[2,8,512]{2,1,0:T(8,128)S(1)} collective-permute-done((f32[2,8,512]{2,1,0:T(8,128)S(1)}, f32[2,8,512]{2,1,0:T(8,128)S(1)}, u32[]{:S(2)}, u32[]{:S(2)}) %collective-permute-start.9) | collective-permute-done | bytes 32800 | tf_op jit(solution)/shard_map/ppermute | solution.py:526
  93.8 1.9 %collective-permute-start.10 = (f32[2,8,512]{2,1,0:T(8,128)S(1)}, f32[2,8,512]{2,1,0:T(8,128)S(1)}, u32[]{:S(2)}, u32[]{:S(2)}) collective-permute-start(f32[2,8,512]{2,1,0:T(8,128)S(1)} %shard_map.54.one_ref), channel_id=1, source_target_pairs={{0,2},{1,3},{2,0},{3,1},{4,6},{5,7},{6,4},{7,5},{8,10},{9,11},{10,... | collective-permute-start | bytes 98312 | tf_op jit(solution)/shard_map/ppermute | solution.py:526
  95.7 2.1 %collective-permute-done.10.two_ref = f32[2,8,512]{2,1,0:T(8,128)S(1)} collective-permute-done((f32[2,8,512]{2,1,0:T(8,128)S(1)}, f32[2,8,512]{2,1,0:T(8,128)S(1)}, u32[]{:S(2)}, u32[]{:S(2)}) %collective-permute-start.10) | collective-permute-done | bytes 32800 | tf_op jit(solution)/shard_map/ppermute | solution.py:526
  97.8 2.9 %collective-permute-start.11 = (f32[2,8,512]{2,1,0:T(8,128)S(1)}, f32[2,8,512]{2,1,0:T(8,128)S(1)}, u32[]{:S(2)}, u32[]{:S(2)}) collective-permute-start(f32[2,8,512]{2,1,0:T(8,128)S(1)} %shard_map.55.stat_ref.refs_4_.one_ref), channel_id=1, source_target_pairs={{0,4},{1,5},{2,6},{3,7},{4,0},{5,1},{6,2},{7,3},{8,12},{9,13},{10,... | collective-permute-start | bytes 98312 | tf_op jit(solution)/shard_map/ppermute | solution.py:526
  100.7 2.0 %collective-permute-done.11.more_ref.two_ref = f32[2,8,512]{2,1,0:T(8,128)S(1)} collective-permute-done((f32[2,8,512]{2,1,0:T(8,128)S(1)}, f32[2,8,512]{2,1,0:T(8,128)S(1)}, u32[]{:S(2)}, u32[]{:S(2)}) %collective-permute-start.11) | collective-permute-done | bytes 32800 | tf_op jit(solution)/shard_map/ppermute | solution.py:526
  102.7 8.4 %shard_map.56 = (f32[1,1032,256]{2,1,0:T(8,128)S(1)}, f32[1,1032,256]{2,1,0:T(8,128)S(1)}, bf16[4096,1024]{1,0:T(8,128)(2,1)S(1)}) custom-call(f32[2,8,512]{2,1,0:T(8,128)S(1)} %shard_map.55.stat_ref.refs_4_.one_ref, f32[2,8,512]{2,1,0:T(8,128)S(1)} %collective-permute-done.11.more_ref.two_ref, ...), custom_call_target="tpu_custom_call", output_to_operand_aliasing={{2}: (5, {})} | custom-call | flops 4294967296 | bytes 20971520 | tf_op jit(solution)/shard_map/pallas_call | solution.py:350
  111.0 0.1 collective-permute-start.12
  111.1 8.2 %shard_map.57 = (f32[1,1032,256]{2,1,0:T(8,128)S(1)}, bf16[4096,1024]{1,0:T(8,128)(2,1)S(1)}) custom-call(f32[2,8,512]{2,1,0:T(8,128)S(1)} %shard_map.55.stat_ref.refs_4_.one_ref, f32[2,8,512]{2,1,0:T(8,128)S(1)} %collective-permute-done.11.more_ref.two_ref, ...), custom_call_target="tpu_custom_call", output_to_operand_aliasing={{1}: (5, {})} | custom-call | flops 2147483648 | bytes 18874368 | tf_op jit(solution)/shard_map/pallas_call | solution.py:350
  119.4 0.6 collective-permute-start.13
  119.9 0.0 collective-permute-done.12.theirs_ref
  119.9 0.8 shard_map.58.refs_4_
  120.7 1.8 %collective-permute-start.14 = (bf16[1040,256]{1,0:T(8,128)(2,1)S(1)}, bf16[1040,256]{1,0:T(8,128)(2,1)S(1)}, u32[]{:S(2)}, u32[]{:S(2)}) collective-permute-start(bf16[1040,256]{1,0:T(8,128)(2,1)S(1)} %bitcast.10), channel_id=1, source_target_pairs={{0,16},{8,24},{16,0},{24,8},{1,17},{9,25},{17,1},{25,9},{2,18},{10... | collective-permute-start | bytes 1597448 | tf_op jit(solution)/shard_map/ppermute | solution.py:514
  122.5 0.6 copy.15
  123.1 8.3 %shard_map.59 = (f32[1,1032,256]{2,1,0:T(8,128)S(1)}, bf16[4096,1024]{1,0:T(8,128)(2,1)S(1)}) custom-call(f32[2,8,512]{2,1,0:T(8,128)S(1)} %shard_map.55.stat_ref.refs_4_.one_ref, f32[2,8,512]{2,1,0:T(8,128)S(1)} %collective-permute-done.11.more_ref.two_ref, ...), custom_call_target="tpu_custom_call", output_to_operand_aliasing={{1}: (5, {})} | custom-call | flops 2147483648 | bytes 18874368 | tf_op jit(solution)/shard_map/pallas_call | solution.py:350
  131.4 0.0 collective-permute-done.13
  131.4 3.4 %collective-permute-done.14.refs_0_ = bf16[1040,256]{1,0:T(8,128)(2,1)S(1)} collective-permute-done((bf16[1040,256]{1,0:T(8,128)(2,1)S(1)}, bf16[1040,256]{1,0:T(8,128)(2,1)S(1)}, u32[]{:S(2)}, u32[]{:S(2)}) %collective-permute-start.14) | collective-permute-done | bytes 532512 | tf_op jit(solution)/shard_map/ppermute | solution.py:514
  134.8 2.0 %shard_map.60 = f32[1024,256]{1,0:T(8,128)} custom-call(f32[1032,256]{1,0:T(8,128)S(1)} %bitcast.14, f32[1032,256]{1,0:T(8,128)S(1)} %bitcast.13, bf16[1040,256]{1,0:T(8,128)(2,1)S(1)} %collective-permute-done.14.refs_0_), custom_call_target="tpu_custom_call" | custom-call | flops 7864320 | bytes 3670016 | tf_op jit(solution)/shard_map/pallas_call | solution.py:458
  (7 shorter events, 0.1 us)
Async XLA Ops:
  0.6 3.5 %copy-start = (f32[1024,1024]{1,0:T(8,128)S(1)}, f32[1024,1024]{1,0:T(8,128)}, u32[]{:S(2)}) copy-start(f32[1024,1024]{1,0:T(8,128)} %c_hbm.1) | copy-start | bytes 12582916
  22.1 4.9 %collective-permute-start = (f32[2,8,512]{2,1,0:T(8,128)S(1)}, f32[2,8,512]{2,1,0:T(8,128)S(1)}, u32[]{:S(2)}, u32[]{:S(2)}) collective-permute-start(f32[2,8,512]{2,1,0:T(8,128)S(1)} %get-tuple-element.28.one_ref.refs_0_), channel_id=1, source_target_pairs={{0,1},{1,0},{2,3},{3,2},{4,5},{5,4},{6,7},{7,6},{8,9},{9,8},{10,11... | collective-permute-start | bytes 98312 | tf_op jit(solution)/shard_map/ppermute | solution.py:526
  27.1 4.1 %collective-permute-start.1 = (f32[2,8,512]{2,1,0:T(8,128)S(1)}, f32[2,8,512]{2,1,0:T(8,128)S(1)}, u32[]{:S(2)}, u32[]{:S(2)}) collective-permute-start(f32[2,8,512]{2,1,0:T(8,128)S(1)} %shard_map.43.one_ref), channel_id=1, source_target_pairs={{0,2},{1,3},{2,0},{3,1},{4,6},{5,7},{6,4},{7,5},{8,10},{9,11},{10,... | collective-permute-start | bytes 98312 | tf_op jit(solution)/shard_map/ppermute | solution.py:526
  31.2 5.0 %collective-permute-start.2 = (f32[2,8,512]{2,1,0:T(8,128)S(1)}, f32[2,8,512]{2,1,0:T(8,128)S(1)}, u32[]{:S(2)}, u32[]{:S(2)}) collective-permute-start(f32[2,8,512]{2,1,0:T(8,128)S(1)} %shard_map.44.stat_ref.refs_3_), channel_id=1, source_target_pairs={{0,4},{1,5},{2,6},{3,7},{4,0},{5,1},{6,2},{7,3},{8,12},{9,13},{10,... | collective-permute-start | bytes 98312 | tf_op jit(solution)/shard_map/ppermute | solution.py:526
  43.1 5.0 %collective-permute-start.3 = (f32[1,264,1024]{2,1,0:T(8,128)S(1)}, f32[1,264,1024]{2,1,0:T(8,128)S(1)}, u32[]{:S(2)}, u32[]{:S(2)}) collective-permute-start(f32[1,264,1024]{2,1,0:T(8,128)S(1)} %get-tuple-element.32.refs_3_), channel_id=1, source_target_pairs={{0,8},{8,0},{16,24},{24,16},{1,9},{9,1},{17,25},{25,17},{2,10},{10... | collective-permute-start | bytes 3244040 | tf_op jit(solution)/shard_map/ppermute | solution.py:510
  47.5 7.5 %collective-permute-start.4 = (f32[1,264,1024]{2,1,0:T(8,128)S(1)}, f32[1,264,1024]{2,1,0:T(8,128)S(1)}, u32[]{:S(2)}, u32[]{:S(2)}) collective-permute-start(f32[1,264,1024]{2,1,0:T(8,128)S(1)} %get-tuple-element.35.after_ref), channel_id=1, source_target_pairs={{0,8},{8,0},{16,24},{24,16},{1,9},{9,1},{17,25},{25,17},{2,10},{10... | collective-permute-start | bytes 3244040 | tf_op jit(solution)/shard_map/ppermute | solution.py:510
  48.8 14.7 %collective-permute-start.5 = (bf16[272,1024]{1,0:T(8,128)(2,1)S(1)}, bf16[272,1024]{1,0:T(8,128)(2,1)S(1)}, u32[]{:S(2)}, u32[]{:S(2)}) collective-permute-start(bf16[272,1024]{1,0:T(8,128)(2,1)S(1)} %bitcast.9), channel_id=1, source_target_pairs={{0,16},{8,24},{16,0},{24,8},{1,17},{9,25},{17,1},{25,9},{2,18},{10... | collective-permute-start | bytes 1671176 | tf_op jit(solution)/shard_map/ppermute | solution.py:514
  64.5 2.0 %collective-permute-start.6 = (bf16[256,1024]{1,0:T(8,128)(2,1)S(1)}, bf16[256,1024]{1,0:T(8,128)(2,1)S(1)}, u32[]{:S(2)}, u32[]{:S(2)}) collective-permute-start(bf16[256,1024]{1,0:T(8,128)(2,1)S(1)} %shard_map.49.refs_0_), channel_id=1, source_target_pairs={{0,8},{8,0},{16,24},{24,16},{1,9},{9,1},{17,25},{25,17},{2,10},{10... | collective-permute-start | bytes 1572872 | tf_op jit(solution)/shard_map/ppermute | solution.py:510
  64.5 14.3 %collective-permute-start.7 = (bf16[256,1024]{1,0:T(8,128)(2,1)S(1)}, bf16[256,1024]{1,0:T(8,128)(2,1)S(1)}, u32[]{:S(2)}, u32[]{:S(2)}) collective-permute-start(bf16[256,1024]{1,0:T(8,128)(2,1)S(1)} %shard_map.49.refs_0_), channel_id=1, source_target_pairs={{0,16},{8,24},{16,0},{24,8},{1,17},{9,25},{17,1},{25,9},{2,18},{10... | collective-permute-start | bytes 1572872 | tf_op jit(solution)/shard_map/ppermute | solution.py:514
  78.9 1.9 %collective-permute-start.8 = (bf16[256,1024]{1,0:T(8,128)(2,1)S(1)}, bf16[256,1024]{1,0:T(8,128)(2,1)S(1)}, u32[]{:S(2)}, u32[]{:S(2)}) collective-permute-start(bf16[256,1024]{1,0:T(8,128)(2,1)S(1)} %shard_map.51.refs_0_), channel_id=1, source_target_pairs={{0,8},{8,0},{16,24},{24,16},{1,9},{9,1},{17,25},{25,17},{2,10},{10... | collective-permute-start | bytes 1572872 | tf_op jit(solution)/shard_map/ppermute | solution.py:510
  89.8 4.0 %collective-permute-start.9 = (f32[2,8,512]{2,1,0:T(8,128)S(1)}, f32[2,8,512]{2,1,0:T(8,128)S(1)}, u32[]{:S(2)}, u32[]{:S(2)}) collective-permute-start(f32[2,8,512]{2,1,0:T(8,128)S(1)} %shard_map.53.one_ref), channel_id=1, source_target_pairs={{0,1},{1,0},{2,3},{3,2},{4,5},{5,4},{6,7},{7,6},{8,9},{9,8},{10,11... | collective-permute-start | bytes 98312 | tf_op jit(solution)/shard_map/ppermute | solution.py:526
  93.8 4.0 %collective-permute-start.10 = (f32[2,8,512]{2,1,0:T(8,128)S(1)}, f32[2,8,512]{2,1,0:T(8,128)S(1)}, u32[]{:S(2)}, u32[]{:S(2)}) collective-permute-start(f32[2,8,512]{2,1,0:T(8,128)S(1)} %shard_map.54.one_ref), channel_id=1, source_target_pairs={{0,2},{1,3},{2,0},{3,1},{4,6},{5,7},{6,4},{7,5},{8,10},{9,11},{10,... | collective-permute-start | bytes 98312 | tf_op jit(solution)/shard_map/ppermute | solution.py:526
  97.8 4.9 %collective-permute-start.11 = (f32[2,8,512]{2,1,0:T(8,128)S(1)}, f32[2,8,512]{2,1,0:T(8,128)S(1)}, u32[]{:S(2)}, u32[]{:S(2)}) collective-permute-start(f32[2,8,512]{2,1,0:T(8,128)S(1)} %shard_map.55.stat_ref.refs_4_.one_ref), channel_id=1, source_target_pairs={{0,4},{1,5},{2,6},{3,7},{4,0},{5,1},{6,2},{7,3},{8,12},{9,13},{10,... | collective-permute-start | bytes 98312 | tf_op jit(solution)/shard_map/ppermute | solution.py:526
  111.0 8.9 %collective-permute-start.12 = (f32[1,1032,256]{2,1,0:T(8,128)S(1)}, f32[1,1032,256]{2,1,0:T(8,128)S(1)}, u32[]{:S(2)}, u32[]{:S(2)}) collective-permute-start(f32[1,1032,256]{2,1,0:T(8,128)S(1)} %get-tuple-element.45.refs_4_), channel_id=1, source_target_pairs={{0,8},{8,0},{16,24},{24,16},{1,9},{9,1},{17,25},{25,17},{2,10},{10... | collective-permute-start | bytes 3170312 | tf_op jit(solution)/shard_map/ppermute | solution.py:510
  119.4 12.0 %collective-permute-start.13 = (f32[1,1032,256]{2,1,0:T(8,128)S(1)}, f32[1,1032,256]{2,1,0:T(8,128)S(1)}, u32[]{:S(2)}, u32[]{:S(2)}) collective-permute-start(f32[1,1032,256]{2,1,0:T(8,128)S(1)} %get-tuple-element.48.after_ref), channel_id=1, source_target_pairs={{0,8},{8,0},{16,24},{24,16},{1,9},{9,1},{17,25},{25,17},{2,10},{10... | collective-permute-start | bytes 3170312 | tf_op jit(solution)/shard_map/ppermute | solution.py:510
  120.7 14.1 %collective-permute-start.14 = (bf16[1040,256]{1,0:T(8,128)(2,1)S(1)}, bf16[1040,256]{1,0:T(8,128)(2,1)S(1)}, u32[]{:S(2)}, u32[]{:S(2)}) collective-permute-start(bf16[1040,256]{1,0:T(8,128)(2,1)S(1)} %bitcast.10), channel_id=1, source_target_pairs={{0,16},{8,24},{16,0},{24,8},{1,17},{9,25},{17,1},{25,9},{2,18},{10... | collective-permute-start | bytes 1597448 | tf_op jit(solution)/shard_map/ppermute | solution.py:514

commit v4 on v3

--- a/solution.py
+++ b/solution.py
@@ -48,9 +48,15 @@
 ANY = pl.BlockSpec(memory_space=pl.ANY)
 
 
-def merge(stats, other):
-    top = jnp.maximum(stats[0], other[0])
-    return top, stats[1] * jnp.exp(stats[0] - top) + other[1] * jnp.exp(other[0] - top)
+def merge(found):
+    found = list(found)
+    top = functools.reduce(jnp.maximum, [stats[0] for stats in found])
+    total = functools.reduce(jnp.add, [stats[1] * jnp.exp(stats[0] - top) for stats in found])
+    return top, total
+
+
+def split(ref):
+    return [(ref[i, 0], ref[i, 1]) for i in range(ref.shape[0])]
 
 
 def to_column(row, height):
@@ -234,14 +240,14 @@
 FAR, THEIRS, OWN = range(3)
 
 
-def weigh_body(by_rows, n_tops, kind, others, extra, pair, stat_ref, more_ref, *refs):
+def weigh_body(by_rows, n_tops, kind, others, extra, pair, stat_ref, *refs):
     parts = CORES if kind == FAR else 1
     top_refs, (e_hbm, x_ref, _), refs = refs[:n_tops], refs[n_tops : n_tops + 3], refs[n_tops + 3 :]
     out_refs, refs = refs[:parts], refs[parts + 1 :]
     scale_refs, refs = refs[:2], refs[2:]
     weights_refs, (stage, mass_ref, sum_ref, semaphores) = refs[:2], refs[2:]
     chip, core = place()
-    line = stat_ref.shape[2]
+    line = stat_ref.shape[3]
     total = x_ref.shape[0]
     height, span = sum_ref.shape
     slots, _, chunk = stage.shape
@@ -262,7 +268,7 @@
 
     for number in range(min(slots, others * steps)):
         copy_of(number).start()
-    top, all_total = merge(stat_ref, more_ref)
+    top, all_total = merge(split(stat_ref))
     if by_rows:
         scale_refs[0][...] = top
         scale_refs[1][...] = 1.0 / all_total
@@ -337,7 +343,7 @@
     total, width = points.shape
     pair = shifted.shape[0] // chips
     parts, others = (CORES, chips - 1) if kind == FAR else (1, 1)
-    line = stats[0].shape[2]
+    line = stats.shape[3]
     chunk = line * divisor(total // line, 2)
     if by_rows:
         rows, cols = pair // CORES, width
@@ -349,10 +355,10 @@
     extra = round_up(-(-rows // cols), 8)
     return pl.pallas_call(
         functools.partial(weigh_body, by_rows, n_tops, kind, others, extra, pair),
-        in_specs=[VMEM] * (2 + n_tops) + [ANY, VMEM, ANY],
+        in_specs=[VMEM] * (1 + n_tops) + [ANY, VMEM, ANY],
         out_specs=[VMEM] * (parts + 1),
-        input_output_aliases={3 + n_tops: parts},
-        scratch_shapes=[pltpu.VMEM(stats[0].shape[1:], F32)] * 2
+        input_output_aliases={2 + n_tops: parts},
+        scratch_shapes=[pltpu.VMEM(stats.shape[2:], F32)] * 2
         + [pltpu.VMEM((sums[0], chunk), BF16)] * 2
         + [
             pltpu.VMEM((2, sums[0], chunk), F32),
@@ -368,7 +374,7 @@
             bytes_accessed=2 * others * total * (sums[1] + 2 * sums[0]),
             transcendentals=0,
         ),
-    )(*stats, *tops, shifted, points, after)
+    )(stats, *tops, shifted, points, after)
 
 
 def fold_body(rows, lines, mine_ref, theirs_ref, after_ref, out_ref):
@@ -483,7 +489,7 @@
 
 
 def merge_body(one_ref, two_ref, out_ref):
-    out_ref[0], out_ref[1] = merge(one_ref, two_ref)
+    out_ref[0], out_ref[1] = merge([one_ref, two_ref])
 
 
 def merged(one, two):
@@ -492,15 +498,15 @@
     )(one, two)
 
 
-def log_body(one_ref, two_ref, out_ref):
-    top, total = merge(one_ref, two_ref)
+def log_body(stats_ref, out_ref):
+    top, total = merge(split(stats_ref))
     out_ref[...] = top + jnp.log(total)
 
 
-def log_norms(one, two):
-    return pl.pallas_call(
-        log_body, out_shape=jax.ShapeDtypeStruct(one.shape[1:], F32), compiler_params=params(10)
-    )(one, two).reshape(-1)
+def log_norms(stats):
+    return pl.pallas_call(
+        log_body, out_shape=jax.ShapeDtypeStruct(stats.shape[2:], F32), compiler_params=params(10)
+    )(stats).reshape(-1)
 
 
 def on_device(n_pts, n_cen, points, centroids):
@@ -514,20 +520,7 @@
         return lax.ppermute(value, "pts", moves)
 
     def over_centroids(stats):
-        if n_cen & (n_cen - 1):
-            found = [stats]
-            for away in range(1, n_cen):
-                moves = [(i, (i + away) % n_cen) for i in range(n_cen)]
-                found.append(lax.ppermute(stats, "cen", moves))
-            return functools.reduce(merged, found[:-1]), found[-1]
-        away = 1
-        while True:
-            moves = [(i, i ^ away) for i in range(n_cen)]
-            other = lax.ppermute(stats, "cen", moves)
-            away *= 2
-            if away >= n_cen:
-                return stats, other
-            stats = merged(stats, other)
+        return lax.all_to_all(jnp.broadcast_to(stats[None], (n_cen, *stats.shape)), "cen", 0, 0)
 
     def sums_over_pts(by_rows, stats, tops, shifted, points):
         def weighted(kind, after):
@@ -535,7 +528,7 @@
             *found, points = weigh(by_rows, kind, chips, stats, tops, shifted, points, after)
             return found
 
-        far_mine, far_theirs = weighted(FAR, stats[0])
+        far_mine, far_theirs = weighted(FAR, stats)
         far_found = to_partner(far_theirs)
         (near_theirs,) = weighted(THEIRS, far_theirs)
         near_found = to_partner(near_theirs)
@@ -559,7 +552,7 @@
         tops = [near_own, far_own]
         stats = over_centroids(merged(near_own, far_own))
     means, _ = sums_over_pts(False, stats, tops, shifted, points)
-    return (means, log_norms(*stats))
+    return (means, log_norms(stats))
 
 
 def solution(mesh):

time: 137 us -> 139 us (1.015)
  blocking collectives: 0 us -> 28.6 us
  starting transfers between devices: 21.7 us -> 6.11 us
  waiting for transfers between devices: 29.1 us -> 17.7 us
    all_to_all x0 -> x2, blocking collectives: none -> 28.6 us  [over_centroids(): lax.all_to_all(jnp.broadcast_to(stats[None], (n_cen, *stats.shape)), 'cen...]
    ppermute x6 -> x0, starting transfers between devices: 14.9 us -> none  [over_centroids(): other = lax.ppermute(stats, 'cen', moves)]
    ppermute x6 -> x0, waiting for transfers between devices: 12 us -> none  [over_centroids(): other = lax.ppermute(stats, 'cen', moves)]
  transfers between devices with their start and end apart: 15 -> 9, of which waited for: 11 -> 5; matrix products, arithmetic and copies ran while one was open for 0% -> 0% of each run, Pallas kernels for 26% -> 26%
where the time goes in v4:
time: 139 us
  Pallas kernels  81.2 us (58%)
  blocking collectives  28.6 us (21%)
  waiting for transfers between devices  17.7 us (13%)
  starting transfers between devices  6.11 us (4%)
  other arithmetic  2.68 us (2%)
  local copies, waits for them, and re-layouts  1.41 us (1%)
    pallas_call x6, Pallas kernels, weigh(): pl.pallas_call(functools.partial(weigh_body, by_rows, n_tops, kind, other...  40.5 us
    pallas_call x3, Pallas kernels, scores(): pl.pallas_call(body, in_specs=[VMEM] * (count + 1) + [ANY] * len(more), o...  32.5 us
    all_to_all x2, blocking collectives, over_centroids(): lax.all_to_all(jnp.broadcast_to(stats[None], (n_cen, *stats.shape)), 'cen...  28.6 us
    ppermute x3, waiting for transfers between devices, to_chip(): return lax.ppermute(value, 'pts', moves)  15.5 us
    ppermute x3, starting transfers between devices, to_chip(): return lax.ppermute(value, 'pts', moves)  4.74 us
    pallas_call x1, Pallas kernels, load(): pl.pallas_call(load_body, in_specs=[ANY, VMEM, ANY], out_specs=[VMEM] * 2...  3.7 us
    pallas_call x2, Pallas kernels, finish(): pl.pallas_call(functools.partial(finish_body, rows, lines, as_units), out...  2.97 us
  transfers between devices with their start and end apart: 9, of which 5 were waited for; matrix products, arithmetic and copies ran while one was open for 0% of the time, Pallas kernels for 26%

profile of v4, /device:TPU:0, one launch (start us, length us, event | category | flops | bytes accessed | tf_op | source)
XLA Modules:
  0.0 138.5 jit_solution(13951831445626224962)
XLA Ops:
  0.6 0.0 copy-start
  0.6 2.7 %multiply_reduce_fusion = f32[1024]{0:T(1024)S(1)} fusion(f32[1024,1024]{1,0:T(8,128)} %c_hbm.1), kind=kLoop, calls=%fused_computation | loop fusion | flops 2096128 | bytes 4198400 | tf_op jit(solution)/shard_map/reduce_sum | solution.py:101
  3.3 0.8 copy-done
  4.1 3.7 %shard_map.41 = (bf16[4096,1024]{1,0:T(8,128)(2,1)S(1)}, bf16[1024,1024]{1,0:T(8,128)(2,1)S(1)}) custom-call(f32[1024,1024]{1,0:T(8,128)S(1)} %copy-done, f32[1,1024]{1,0:T(1,128)S(1)} %bitcast.16, bf16[4096,1024]{1,0:T(8,128)(2,1)} %x_hbm.1), custom_call_target="tpu_custom_call" | custom-call | flops 4194304 | bytes 12582912 | tf_op jit(solution)/shard_map/pallas_call | solution.py:102
  7.8 14.4 %shard_map.42 = (bf16[4096,1024]{1,0:T(8,128)(2,1)S(1)}, f32[1024,4096]{1,0:T(8,128)}, f32[2,8,512]{2,1,0:T(8,128)S(1)}) custom-call(bf16[1024,1024]{1,0:T(8,128)(2,1)S(1)} %get-tuple-element.26.units, bf16[4096,1024]{1,0:T(8,128)(2,1)S(1)} %get-tuple-element.27.x_ref), custom_call_target="tpu_custom_call", output_to_operand_aliasing={{0}: (1, {})} | custom-call | flops 8589934592 | bytes 25165824 | tf_op jit(solution)/shard_map/pallas_call | solution.py:220
  22.2 16.0 %all_to_all.10.stat_ref.refs_3_ = f32[8,2,8,512]{3,2,1,0:T(8,128)S(1)} all-to-all(f32[8,2,8,512]{3,2,1,0:T(8,128)S(1)} %broadcast_in_dim.7), channel_id=1, replica_groups=mesh['pts'=4,'cen'=8] {'cen'}, dimensions={0} | all-to-all | bytes 524288 | tf_op jit(solution)/shard_map/all_to_all | solution.py:523
  38.2 6.9 %shard_map.43 = (f32[1,264,1024]{2,1,0:T(8,128)S(1)}, f32[1,264,1024]{2,1,0:T(8,128)S(1)}, bf16[4096,1024]{1,0:T(8,128)(2,1)S(1)}) custom-call(f32[8,2,8,512]{3,2,1,0:T(8,128)S(1)} %all_to_all.10.stat_ref.refs_3_, f32[2,8,512]{2,1,0:T(8,128)S(1)} %get-tuple-element.28.refs_0_, ...), custom_call_target="tpu_custom_call", output_to_operand_aliasing={{2}: (3, {})} | custom-call | flops 4294967296 | bytes 16777216 | tf_op jit(solution)/shard_map/pallas_call | solution.py:356
  45.1 0.1 collective-permute-start
  45.2 4.4 %shard_map.44 = (f32[1,264,1024]{2,1,0:T(8,128)S(1)}, bf16[4096,1024]{1,0:T(8,128)(2,1)S(1)}) custom-call(f32[8,2,8,512]{3,2,1,0:T(8,128)S(1)} %all_to_all.10.stat_ref.refs_3_, f32[2,8,512]{2,1,0:T(8,128)S(1)} %get-tuple-element.28.refs_0_, f32[1024,4096]{1,0:T(8,128)} %get-tuple-element.29.refs_1_, ...), custom_call_target="tpu_custom_call", output_to_operand_aliasing={{1}: (3, {})} | custom-call | flops 2147483648 | bytes 12582912 | tf_op jit(solution)/shard_map/pallas_call | solution.py:356
  49.6 0.6 collective-permute-start.1
  50.1 0.0 collective-permute-done.theirs_ref
  50.1 0.7 shard_map.45.refs_3_
  50.8 1.6 %collective-permute-start.2 = (bf16[272,1024]{1,0:T(8,128)(2,1)S(1)}, bf16[272,1024]{1,0:T(8,128)(2,1)S(1)}, u32[]{:S(2)}, u32[]{:S(2)}) collective-permute-start(bf16[272,1024]{1,0:T(8,128)(2,1)S(1)} %bitcast.9), channel_id=1, source_target_pairs={{0,16},{8,24},{16,0},{24,8},{1,17},{9,25},{17,1},{25,9},{2,18},{10... | collective-permute-start | bytes 1671176 | tf_op jit(solution)/shard_map/ppermute | solution.py:520
  52.4 4.4 %shard_map.46 = (f32[1,264,1024]{2,1,0:T(8,128)S(1)}, bf16[4096,1024]{1,0:T(8,128)(2,1)S(1)}) custom-call(f32[8,2,8,512]{3,2,1,0:T(8,128)S(1)} %all_to_all.10.stat_ref.refs_3_, f32[2,8,512]{2,1,0:T(8,128)S(1)} %get-tuple-element.28.refs_0_, f32[1024,4096]{1,0:T(8,128)} %get-tuple-element.29.refs_1_, ...), custom_call_target="tpu_custom_call", output_to_operand_aliasing={{1}: (3, {})} | custom-call | flops 2147483648 | bytes 12582912 | tf_op jit(solution)/shard_map/pallas_call | solution.py:356
  56.8 0.0 collective-permute-done.1
  56.8 8.6 %collective-permute-done.2.refs_0_ = bf16[272,1024]{1,0:T(8,128)(2,1)S(1)} collective-permute-done((bf16[272,1024]{1,0:T(8,128)(2,1)S(1)}, bf16[272,1024]{1,0:T(8,128)(2,1)S(1)}, u32[]{:S(2)}, u32[]{:S(2)}) %collective-permute-start.2) | collective-permute-done | bytes 557088 | tf_op jit(solution)/shard_map/ppermute | solution.py:520
  65.4 0.9 shard_map.47.refs_0_
  66.4 0.1 collective-permute-start.3
  66.5 1.6 %collective-permute-start.4 = (bf16[256,1024]{1,0:T(8,128)(2,1)S(1)}, bf16[256,1024]{1,0:T(8,128)(2,1)S(1)}, u32[]{:S(2)}, u32[]{:S(2)}) collective-permute-start(bf16[256,1024]{1,0:T(8,128)(2,1)S(1)} %shard_map.47.refs_0_), channel_id=1, source_target_pairs={{0,16},{8,24},{16,0},{24,8},{1,17},{9,25},{17,1},{25,9},{2,18},{10... | collective-permute-start | bytes 1572872 | tf_op jit(solution)/shard_map/ppermute | solution.py:520
  68.1 0.3 collective-permute-done.3.refs_1_
  68.4 9.2 %shard_map.48 = (bf16[4096,1024]{1,0:T(8,128)(2,1)S(1)}, f32[1024,4096]{1,0:T(8,128)}, f32[2,8,512]{2,1,0:T(8,128)S(1)}) custom-call(bf16[256,1024]{1,0:T(8,128)(2,1)S(1)} %shard_map.47.refs_0_, bf16[256,1024]{1,0:T(8,128)(2,1)S(1)} %collective-permute-done.3.refs_1_, bf16[4096,1024]{1,0:T(8,128)(2,1)S(1)} %get-tuple-element.37.refs_2_), custom_call_target="tpu_custom_call", output_to_operand_aliasing={{0}: (2, {})} | custom-call | flops 4294967296 | bytes 16777216 | tf_op jit(solution)/shard_map/pallas_call | solution.py:220
  77.5 3.3 %collective-permute-done.4.value_ref = bf16[256,1024]{1,0:T(8,128)(2,1)S(1)} collective-permute-done((bf16[256,1024]{1,0:T(8,128)(2,1)S(1)}, bf16[256,1024]{1,0:T(8,128)(2,1)S(1)}, u32[]{:S(2)}, u32[]{:S(2)}) %collective-permute-start.4) | collective-permute-done | bytes 524320 | tf_op jit(solution)/shard_map/ppermute | solution.py:520
  80.8 0.0 collective-permute-start.5
  80.8 1.9 %collective-permute-done.5.refs_1_ = bf16[256,1024]{1,0:T(8,128)(2,1)S(1)} collective-permute-done((bf16[256,1024]{1,0:T(8,128)(2,1)S(1)}, bf16[256,1024]{1,0:T(8,128)(2,1)S(1)}, u32[]{:S(2)}, u32[]{:S(2)}) %collective-permute-start.5) | collective-permute-done | bytes 524320 | tf_op jit(solution)/shard_map/ppermute | solution.py:516
  82.7 9.0 %shard_map.50 = (bf16[4096,1024]{1,0:T(8,128)(2,1)S(1)}, f32[1024,4096]{1,0:T(8,128)}, f32[2,8,512]{2,1,0:T(8,128)S(1)}) custom-call(bf16[256,1024]{1,0:T(8,128)(2,1)S(1)} %shard_map.49.refs_0_, bf16[256,1024]{1,0:T(8,128)(2,1)S(1)} %collective-permute-done.5.refs_1_, ...), custom_call_target="tpu_custom_call", output_to_operand_aliasing={{0}: (2, {}), {1}: (3, {})} | custom-call | flops 4294967296 | bytes 16777216 | tf_op jit(solution)/shard_map/pallas_call | solution.py:220
  91.7 12.6 %all_to_all.11.stat_ref.refs_4_.stats_ref = f32[8,2,8,512]{3,2,1,0:T(8,128)S(1)} all-to-all(f32[8,2,8,512]{3,2,1,0:T(8,128)S(1)} %broadcast_in_dim.8), channel_id=1, replica_groups=mesh['pts'=4,'cen'=8] {'cen'}, dimensions={0} | all-to-all | bytes 524288 | tf_op jit(solution)/shard_map/all_to_all | solution.py:523
  104.3 8.4 %shard_map.52 = (f32[1,1032,256]{2,1,0:T(8,128)S(1)}, f32[1,1032,256]{2,1,0:T(8,128)S(1)}, bf16[4096,1024]{1,0:T(8,128)(2,1)S(1)}) custom-call(f32[8,2,8,512]{3,2,1,0:T(8,128)S(1)} %all_to_all.11.stat_ref.refs_4_.stats_ref, f32[2,8,512]{2,1,0:T(8,128)S(1)} %get-tuple-element.38.after_ref.one_ref.refs_0_, ...), custom_call_target="tpu_custom_call", output_to_operand_aliasing={{2}: (4, {})} | custom-call | flops 4294967296 | bytes 20971520 | tf_op jit(solution)/shard_map/pallas_call | solution.py:356
  112.7 0.1 collective-permute-start.6
  112.8 8.2 %shard_map.53 = (f32[1,1032,256]{2,1,0:T(8,128)S(1)}, bf16[4096,1024]{1,0:T(8,128)(2,1)S(1)}) custom-call(f32[8,2,8,512]{3,2,1,0:T(8,128)S(1)} %all_to_all.11.stat_ref.refs_4_.stats_ref, f32[2,8,512]{2,1,0:T(8,128)S(1)} %get-tuple-element.38.after_ref.one_ref.refs_0_, ...), custom_call_target="tpu_custom_call", output_to_operand_aliasing={{1}: (4, {})} | custom-call | flops 2147483648 | bytes 18874368 | tf_op jit(solution)/shard_map/pallas_call | solution.py:356
  121.0 0.6 collective-permute-start.7
  121.6 0.0 collective-permute-done.6.theirs_ref
  121.6 0.8 shard_map.54.refs_4_
  122.4 1.6 %collective-permute-start.8 = (bf16[1040,256]{1,0:T(8,128)(2,1)S(1)}, bf16[1040,256]{1,0:T(8,128)(2,1)S(1)}, u32[]{:S(2)}, u32[]{:S(2)}) collective-permute-start(bf16[1040,256]{1,0:T(8,128)(2,1)S(1)} %bitcast.10), channel_id=1, source_target_pairs={{0,16},{8,24},{16,0},{24,8},{1,17},{9,25},{17,1},{25,9},{2,18},{10... | collective-permute-start | bytes 1597448 | tf_op jit(solution)/shard_map/ppermute | solution.py:520
  124.0 0.6 copy.15
  124.6 8.3 %shard_map.55 = (f32[1,1032,256]{2,1,0:T(8,128)S(1)}, bf16[4096,1024]{1,0:T(8,128)(2,1)S(1)}) custom-call(f32[8,2,8,512]{3,2,1,0:T(8,128)S(1)} %all_to_all.11.stat_ref.refs_4_.stats_ref, f32[2,8,512]{2,1,0:T(8,128)S(1)} %get-tuple-element.38.after_ref.one_ref.refs_0_, ...), custom_call_target="tpu_custom_call", output_to_operand_aliasing={{1}: (4, {})} | custom-call | flops 2147483648 | bytes 18874368 | tf_op jit(solution)/shard_map/pallas_call | solution.py:356
  132.9 0.0 collective-permute-done.7
  132.9 3.6 %collective-permute-done.8.refs_0_ = bf16[1040,256]{1,0:T(8,128)(2,1)S(1)} collective-permute-done((bf16[1040,256]{1,0:T(8,128)(2,1)S(1)}, bf16[1040,256]{1,0:T(8,128)(2,1)S(1)}, u32[]{:S(2)}, u32[]{:S(2)}) %collective-permute-start.8) | collective-permute-done | bytes 532512 | tf_op jit(solution)/shard_map/ppermute | solution.py:520
  136.5 2.0 %shard_map.56 = f32[1024,256]{1,0:T(8,128)} custom-call(f32[1032,256]{1,0:T(8,128)S(1)} %bitcast.14, f32[1032,256]{1,0:T(8,128)S(1)} %bitcast.13, bf16[1040,256]{1,0:T(8,128)(2,1)S(1)} %collective-permute-done.8.refs_0_), custom_call_target="tpu_custom_call" | custom-call | flops 7864320 | bytes 3670016 | tf_op jit(solution)/shard_map/pallas_call | solution.py:464
  (5 shorter events, 0.1 us)
Async XLA Ops:
  0.6 3.5 %copy-start = (f32[1024,1024]{1,0:T(8,128)S(1)}, f32[1024,1024]{1,0:T(8,128)}, u32[]{:S(2)}) copy-start(f32[1024,1024]{1,0:T(8,128)} %c_hbm.1) | copy-start | bytes 12582916
  45.1 5.0 %collective-permute-start = (f32[1,264,1024]{2,1,0:T(8,128)S(1)}, f32[1,264,1024]{2,1,0:T(8,128)S(1)}, u32[]{:S(2)}, u32[]{:S(2)}) collective-permute-start(f32[1,264,1024]{2,1,0:T(8,128)S(1)} %get-tuple-element.32.refs_3_), channel_id=1, source_target_pairs={{0,8},{8,0},{16,24},{24,16},{1,9},{9,1},{17,25},{25,17},{2,10},{10... | collective-permute-start | bytes 3244040 | tf_op jit(solution)/shard_map/ppermute | solution.py:516
  49.6 7.2 %collective-permute-start.1 = (f32[1,264,1024]{2,1,0:T(8,128)S(1)}, f32[1,264,1024]{2,1,0:T(8,128)S(1)}, u32[]{:S(2)}, u32[]{:S(2)}) collective-permute-start(f32[1,264,1024]{2,1,0:T(8,128)S(1)} %get-tuple-element.35.after_ref), channel_id=1, source_target_pairs={{0,8},{8,0},{16,24},{24,16},{1,9},{9,1},{17,25},{25,17},{2,10},{10... | collective-permute-start | bytes 3244040 | tf_op jit(solution)/shard_map/ppermute | solution.py:516
  50.8 14.6 %collective-permute-start.2 = (bf16[272,1024]{1,0:T(8,128)(2,1)S(1)}, bf16[272,1024]{1,0:T(8,128)(2,1)S(1)}, u32[]{:S(2)}, u32[]{:S(2)}) collective-permute-start(bf16[272,1024]{1,0:T(8,128)(2,1)S(1)} %bitcast.9), channel_id=1, source_target_pairs={{0,16},{8,24},{16,0},{24,8},{1,17},{9,25},{17,1},{25,9},{2,18},{10... | collective-permute-start | bytes 1671176 | tf_op jit(solution)/shard_map/ppermute | solution.py:520
  66.4 2.0 %collective-permute-start.3 = (bf16[256,1024]{1,0:T(8,128)(2,1)S(1)}, bf16[256,1024]{1,0:T(8,128)(2,1)S(1)}, u32[]{:S(2)}, u32[]{:S(2)}) collective-permute-start(bf16[256,1024]{1,0:T(8,128)(2,1)S(1)} %shard_map.47.refs_0_), channel_id=1, source_target_pairs={{0,8},{8,0},{16,24},{24,16},{1,9},{9,1},{17,25},{25,17},{2,10},{10... | collective-permute-start | bytes 1572872 | tf_op jit(solution)/shard_map/ppermute | solution.py:516
  66.5 14.3 %collective-permute-start.4 = (bf16[256,1024]{1,0:T(8,128)(2,1)S(1)}, bf16[256,1024]{1,0:T(8,128)(2,1)S(1)}, u32[]{:S(2)}, u32[]{:S(2)}) collective-permute-start(bf16[256,1024]{1,0:T(8,128)(2,1)S(1)} %shard_map.47.refs_0_), channel_id=1, source_target_pairs={{0,16},{8,24},{16,0},{24,8},{1,17},{9,25},{17,1},{25,9},{2,18},{10... | collective-permute-start | bytes 1572872 | tf_op jit(solution)/shard_map/ppermute | solution.py:520
  80.8 1.9 %collective-permute-start.5 = (bf16[256,1024]{1,0:T(8,128)(2,1)S(1)}, bf16[256,1024]{1,0:T(8,128)(2,1)S(1)}, u32[]{:S(2)}, u32[]{:S(2)}) collective-permute-start(bf16[256,1024]{1,0:T(8,128)(2,1)S(1)} %shard_map.49.refs_0_), channel_id=1, source_target_pairs={{0,8},{8,0},{16,24},{24,16},{1,9},{9,1},{17,25},{25,17},{2,10},{10... | collective-permute-start | bytes 1572872 | tf_op jit(solution)/shard_map/ppermute | solution.py:516
  112.7 8.9 %collective-permute-start.6 = (f32[1,1032,256]{2,1,0:T(8,128)S(1)}, f32[1,1032,256]{2,1,0:T(8,128)S(1)}, u32[]{:S(2)}, u32[]{:S(2)}) collective-permute-start(f32[1,1032,256]{2,1,0:T(8,128)S(1)} %get-tuple-element.45.refs_4_), channel_id=1, source_target_pairs={{0,8},{8,0},{16,24},{24,16},{1,9},{9,1},{17,25},{25,17},{2,10},{10... | collective-permute-start | bytes 3170312 | tf_op jit(solution)/shard_map/ppermute | solution.py:516
  121.0 11.8 %collective-permute-start.7 = (f32[1,1032,256]{2,1,0:T(8,128)S(1)}, f32[1,1032,256]{2,1,0:T(8,128)S(1)}, u32[]{:S(2)}, u32[]{:S(2)}) collective-permute-start(f32[1,1032,256]{2,1,0:T(8,128)S(1)} %get-tuple-element.48.after_ref), channel_id=1, source_target_pairs={{0,8},{8,0},{16,24},{24,16},{1,9},{9,1},{17,25},{25,17},{2,10},{10... | collective-permute-start | bytes 3170312 | tf_op jit(solution)/shard_map/ppermute | solution.py:516
  122.4 14.1 %collective-permute-start.8 = (bf16[1040,256]{1,0:T(8,128)(2,1)S(1)}, bf16[1040,256]{1,0:T(8,128)(2,1)S(1)}, u32[]{:S(2)}, u32[]{:S(2)}) collective-permute-start(bf16[1040,256]{1,0:T(8,128)(2,1)S(1)} %bitcast.10), channel_id=1, source_target_pairs={{0,16},{8,24},{16,0},{24,8},{1,17},{9,25},{17,1},{25,9},{2,18},{10... | collective-permute-start | bytes 1597448 | tf_op jit(solution)/shard_map/ppermute | solution.py:520
